TPU v7x, 32 devices: a whole 2x2x4 slice. The times are simulated.
32 devices in a mesh: dp: 8 (over z, y), tensor: 4 (over x, core).
Axes of the slice: x: 2, y: 2, z: 4, core: 2. Of those that a mesh axis runs over, the one named last changes fastest.
Arguments:
- hidden_in: bfloat16 [8192, 1536], P(('dp', 'tensor')), may hold values from -6 to 6
- segments: int32 [8192], P('dp'), may hold values from 0 to 4, as said below
- attn_gain: bfloat16 [1536], P('dp'), may hold values from 0.25 to 1.75
- w_query: bfloat16 [1536, 1536], P('dp', 'tensor'), may hold values from -0.21875 to 0.21875
- w_key: bfloat16 [1536, 768], P('dp', 'tensor'), may hold values from -0.21875 to 0.21875
- w_value: bfloat16 [1536, 768], P('dp', 'tensor'), may hold values from -0.15625 to 0.15625
- w_out: bfloat16 [1536, 1536], P('tensor', 'dp'), may hold values from -0.4375 to 0.4375
- mlp_gain: bfloat16 [1536], P('dp'), may hold values from 0.25 to 1.75
- w_gate: bfloat16 [1536, 4096], P('dp', 'tensor'), may hold values from -0.15625 to 0.15625
- w_up: bfloat16 [1536, 4096], P('dp', 'tensor'), may hold values from -0.15625 to 0.15625
- w_down: bfloat16 [4096, 1536], P('tensor', 'dp'), may hold values from -0.09375 to 0.09375
- cotangent: bfloat16 [8192, 1536], P(('dp', 'tensor')), may hold values from -6 to 6
Outputs:
- mixed: bfloat16 [8192, 1536], P(('dp', 'tensor'))
- hidden_grad: bfloat16 [8192, 1536], P(('dp', 'tensor'))
- attn_gain_grad: float32 [1536], P('dp')
- w_query_grad: float32 [1536, 1536], P('dp', 'tensor')
- w_key_grad: float32 [1536, 768], P('dp', 'tensor')
- w_value_grad: float32 [1536, 768], P('dp', 'tensor')
- w_out_grad: float32 [1536, 1536], P('tensor', 'dp')
- mlp_gain_grad: float32 [1536], P('dp')
- w_gate_grad: float32 [1536, 4096], P('dp', 'tensor')
- w_up_grad: float32 [1536, 4096], P('dp', 'tensor')
- w_down_grad: float32 [4096, 1536], P('tensor', 'dp')
Inputs may be any that keep to these rules, and one draw needn't show every extreme that they name: `segments`: along each sequence of 1024 tokens the segment numbers start at 0, never fall, and rise by one where a new document begins; every sequence holds exactly five documents.
All inputs are finite; a program needn't handle non-finite values.
Results may differ from a plain program's by a relative error of at most 0.02.
Values may be sent and summed in bfloat16 or wider, within the bound.
No kernel may reach another device: no remote copies, remote signals or barrier semaphores. Data moves between devices by JAX's collectives and lax.ppermute only.
A program may use at most 128 MiB of HBM per device.

v0:
```python
import math

import jax
import jax.numpy as jnp
from jax import lax
from jax.sharding import PartitionSpec as P

HD = 96


EPS = 1e-05
NEG = -1e30
THETA = 100000.0


def matmul(left_side, right_side):
    return jnp.dot(left_side, right_side, preferred_element_type=jnp.float32)


def left_t(left_side, right_side):
    return lax.dot_general(
        left_side, right_side, (((0,), (0,)), ((), ())), preferred_element_type=jnp.float32
    )


def right_t(left_side, right_side):
    return lax.dot_general(
        left_side, right_side, (((1,), (1,)), ((), ())), preferred_element_type=jnp.float32
    )


def rope_tables(segment):
    places = jnp.arange(segment.shape[0], dtype=jnp.int32)
    previous = jnp.concatenate([segment[:1] - 1, segment[:-1]])
    opening = jnp.where(segment != previous, places, 0)
    position = (places - lax.cummax(opening, axis=0)).astype(jnp.float32)
    half_dim = HD // 2
    inverse = jnp.exp(-(2.0 * jnp.arange(half_dim, dtype=jnp.float32) / HD) * math.log(THETA))
    angle = position[:, None] * inverse[None, :]
    return (jnp.cos(angle), jnp.sin(angle))


def rotate(values, cosine_table, sine_table):
    half_dim = values.shape[-1] // 2
    first_half = values[..., :half_dim]
    second_half = values[..., half_dim:]
    cosine = cosine_table[:, None, :]
    sine = sine_table[:, None, :]
    return jnp.concatenate(
        [first_half * cosine - second_half * sine, second_half * cosine + first_half * sine],
        axis=-1,
    )


def unrotate(values, cosine_table, sine_table):
    half_dim = values.shape[-1] // 2
    first_half = values[..., :half_dim]
    second_half = values[..., half_dim:]
    cosine = cosine_table[:, None, :]
    sine = sine_table[:, None, :]
    return jnp.concatenate(
        [first_half * cosine + second_half * sine, second_half * cosine - first_half * sine],
        axis=-1,
    )


def inverse_rms(values):
    return lax.rsqrt(jnp.mean(values * values, axis=-1, keepdims=True) + EPS)


def norm_back(upstream, values, inverse, gain):
    scaled = upstream * gain
    grad_values = inverse * scaled - values * inverse * inverse * inverse * jnp.mean(
        scaled * values, axis=-1, keepdims=True
    )
    return (grad_values, jnp.sum(upstream * values * inverse, axis=0))


def scores_of(query_rows, keys_rot, segment, offset):
    row_count = query_rows.shape[0]
    places = jnp.arange(segment.shape[0], dtype=jnp.int32)
    scores = jnp.einsum(
        "qgrd,kgd->grqk", query_rows, keys_rot, preferred_element_type=jnp.float32
    ) * HD ** (-0.5)
    row_segment = lax.dynamic_slice_in_dim(segment, offset, row_count)
    row_place = offset + jnp.arange(row_count, dtype=jnp.int32)
    allowed = (row_segment[:, None] == segment[None, :]) & (places[None, :] <= row_place[:, None])
    return jnp.where(allowed, scores, NEG)


def attend(queries, keys_rot, values, segment, block_rows):
    length = queries.shape[0]

    def one_block(block_index):
        offset = block_index * block_rows
        query_rows = lax.dynamic_slice_in_dim(queries, offset, block_rows)
        scores = scores_of(query_rows, keys_rot, segment, offset)
        log_total = jax.nn.logsumexp(scores, axis=-1)
        probs = jnp.exp(scores - log_total[..., None]).astype(jnp.bfloat16)
        block_out = jnp.einsum("grqk,kgd->qgrd", probs, values, preferred_element_type=jnp.float32)
        return (block_out.astype(jnp.bfloat16), log_total)

    outputs, log_totals = lax.map(one_block, jnp.arange(length // block_rows, dtype=jnp.int32))
    return (outputs.reshape(length, -1), log_totals)


def attend_back(queries, keys_rot, values, grad_heads, log_totals, segment, block_rows):
    length = queries.shape[0]
    scale = HD ** (-0.5)

    def one_block(totals, block_item):
        grad_keys, grad_values = totals
        block_index, log_total = block_item
        offset = block_index * block_rows
        query_rows = lax.dynamic_slice_in_dim(queries, offset, block_rows)
        grad_rows = lax.dynamic_slice_in_dim(grad_heads, offset, block_rows)
        scores = scores_of(query_rows, keys_rot, segment, offset)
        probs = jnp.exp(scores - log_total[..., None])
        grad_probs = jnp.einsum(
            "qgrd,kgd->grqk", grad_rows, values, preferred_element_type=jnp.float32
        )
        inner_sum = jnp.sum(probs * grad_probs, axis=-1, keepdims=True)
        grad_scores = (probs * (grad_probs - inner_sum)).astype(jnp.bfloat16)
        grad_query = (
            jnp.einsum("grqk,kgd->qgrd", grad_scores, keys_rot, preferred_element_type=jnp.float32)
            * scale
        )
        grad_keys = (
            grad_keys
            + jnp.einsum(
                "grqk,qgrd->kgd", grad_scores, query_rows, preferred_element_type=jnp.float32
            )
            * scale
        )
        grad_values = grad_values + jnp.einsum(
            "grqk,qgrd->kgd",
            probs.astype(jnp.bfloat16),
            grad_rows,
            preferred_element_type=jnp.float32,
        )
        return ((grad_keys, grad_values), grad_query)

    empty_grad = jnp.zeros(keys_rot.shape, jnp.float32)
    indices = jnp.arange(length // block_rows, dtype=jnp.int32)
    (grad_keys, grad_values), grad_query = lax.scan(
        one_block, (empty_grad, empty_grad), (indices, log_totals)
    )
    return (grad_query.reshape(queries.shape), grad_keys, grad_values)


def per_device(
    hidden_in,
    segments,
    attn_gain,
    w_query,
    w_key,
    w_value,
    w_out,
    mlp_gain,
    w_gate,
    w_up,
    w_down,
    cotangent,
):
    gathered = (
        lax.all_gather(w_query, "dp", axis=0, tiled=True),
        lax.all_gather(w_key, "dp", axis=0, tiled=True),
        lax.all_gather(w_value, "dp", axis=0, tiled=True),
        lax.all_gather(w_out, "dp", axis=1, tiled=True),
        lax.all_gather(w_gate, "dp", axis=0, tiled=True),
        lax.all_gather(w_up, "dp", axis=0, tiled=True),
        lax.all_gather(w_down, "dp", axis=1, tiled=True),
        lax.all_gather(attn_gain, "dp", axis=0, tiled=True),
        lax.all_gather(mlp_gain, "dp", axis=0, tiled=True),
    )
    hidden = hidden_in.astype(jnp.float32)
    gain_one = gathered[7].astype(jnp.float32)
    gain_two = gathered[8].astype(jnp.float32)
    inverse_one = inverse_rms(hidden)
    normed = lax.all_gather(
        (hidden * inverse_one * gain_one).astype(jnp.bfloat16), "tensor", axis=0, tiled=True
    )
    length = normed.shape[0]
    block_rows = min(512, length)
    cosine_table, sine_table = rope_tables(segments)
    query_heads = gathered[0].shape[1] // HD
    key_heads = gathered[1].shape[1] // HD
    queries = rotate(
        matmul(normed, gathered[0]).reshape(length, query_heads, HD), cosine_table, sine_table
    )
    queries = queries.astype(jnp.bfloat16).reshape(length, key_heads, query_heads // key_heads, HD)
    keys_rot = rotate(
        matmul(normed, gathered[1]).reshape(length, key_heads, HD), cosine_table, sine_table
    ).astype(jnp.bfloat16)
    values = matmul(normed, gathered[2]).astype(jnp.bfloat16).reshape(length, key_heads, HD)
    heads_out, log_totals = attend(queries, keys_rot, values, segments, block_rows)
    resid = hidden + lax.psum_scatter(
        matmul(heads_out, gathered[3]), "tensor", scatter_dimension=0, tiled=True
    )
    inverse_two = inverse_rms(resid)
    normed_two = lax.all_gather(
        (resid * inverse_two * gain_two).astype(jnp.bfloat16), "tensor", axis=0, tiled=True
    )
    gate_pre = matmul(normed_two, gathered[4])
    upward = matmul(normed_two, gathered[5])
    sigmoid_gate = jax.nn.sigmoid(gate_pre)
    silu_gate = gate_pre * sigmoid_gate
    activated = (silu_gate * upward).astype(jnp.bfloat16)
    output = resid + lax.psum_scatter(
        matmul(activated, gathered[6]).astype(jnp.bfloat16),
        "tensor",
        scatter_dimension=0,
        tiled=True,
    ).astype(jnp.float32)
    weights = (
        lax.all_gather(w_query, "dp", axis=0, tiled=True),
        lax.all_gather(w_key, "dp", axis=0, tiled=True),
        lax.all_gather(w_value, "dp", axis=0, tiled=True),
        lax.all_gather(w_out, "dp", axis=1, tiled=True),
        lax.all_gather(w_gate, "dp", axis=0, tiled=True),
        lax.all_gather(w_up, "dp", axis=0, tiled=True),
        lax.all_gather(w_down, "dp", axis=1, tiled=True),
        lax.all_gather(attn_gain, "dp", axis=0, tiled=True),
        lax.all_gather(mlp_gain, "dp", axis=0, tiled=True),
    )
    upstream = cotangent.astype(jnp.float32)
    grad_rows = lax.all_gather(cotangent, "tensor", axis=0, tiled=True)
    grad_down_w = left_t(activated, grad_rows)
    grad_act = right_t(grad_rows, weights[6])
    grad_gate = (grad_act * upward * sigmoid_gate * (1.0 + gate_pre * (1.0 - sigmoid_gate))).astype(
        jnp.bfloat16
    )
    grad_up = (grad_act * silu_gate).astype(jnp.bfloat16)
    grad_gate_w = left_t(normed_two, grad_gate)
    grad_up_w = left_t(normed_two, grad_up)
    grad_normed_two = lax.psum_scatter(
        right_t(grad_gate, weights[4]) + right_t(grad_up, weights[5]),
        "tensor",
        scatter_dimension=0,
        tiled=True,
    )
    grad_norm_two, gain_two_part = norm_back(grad_normed_two, resid, inverse_two, gain_two)
    grad_resid = upstream + grad_norm_two
    mlp_sums = (
        lax.psum_scatter(
            grad_gate_w.astype(jnp.bfloat16), "dp", scatter_dimension=0, tiled=True
        ).astype(jnp.float32),
        lax.psum_scatter(
            grad_up_w.astype(jnp.bfloat16), "dp", scatter_dimension=0, tiled=True
        ).astype(jnp.float32),
        lax.psum_scatter(
            grad_down_w.astype(jnp.bfloat16), "dp", scatter_dimension=1, tiled=True
        ).astype(jnp.float32),
        lax.psum_scatter(
            gain_two_part.astype(jnp.bfloat16), "dp", scatter_dimension=0, tiled=True
        ).astype(jnp.float32),
    )
    grad_branch = lax.all_gather(grad_resid.astype(jnp.bfloat16), "tensor", axis=0, tiled=True)
    grad_out_w = left_t(heads_out, grad_branch)
    grad_heads = right_t(grad_branch, weights[3]).astype(jnp.bfloat16).reshape(queries.shape)
    grad_query, grad_keys, grad_values = attend_back(
        queries, keys_rot, values, grad_heads, log_totals, segments, block_rows
    )
    grad_query = unrotate(grad_query.reshape(length, query_heads, HD), cosine_table, sine_table)
    grad_query = grad_query.astype(jnp.bfloat16).reshape(length, query_heads * HD)
    grad_keys = (
        unrotate(grad_keys, cosine_table, sine_table)
        .astype(jnp.bfloat16)
        .reshape(length, key_heads * HD)
    )
    grad_values = grad_values.astype(jnp.bfloat16).reshape(length, key_heads * HD)
    grad_query_w = left_t(normed, grad_query)
    grad_keys_w = left_t(normed, grad_keys)
    grad_values_w = left_t(normed, grad_values)
    grad_normed = lax.psum_scatter(
        (
            right_t(grad_query, weights[0])
            + right_t(grad_keys, weights[1])
            + right_t(grad_values, weights[2])
        ).astype(jnp.bfloat16),
        "tensor",
        scatter_dimension=0,
        tiled=True,
    ).astype(jnp.float32)
    grad_norm_one, gain_one_part = norm_back(grad_normed, hidden, inverse_one, gain_one)
    hidden_grad = (grad_resid + grad_norm_one).astype(jnp.bfloat16)
    attn_sums = (
        lax.psum_scatter(
            grad_query_w.astype(jnp.bfloat16), "dp", scatter_dimension=0, tiled=True
        ).astype(jnp.float32),
        lax.psum_scatter(
            grad_keys_w.astype(jnp.bfloat16), "dp", scatter_dimension=0, tiled=True
        ).astype(jnp.float32),
        lax.psum_scatter(
            grad_values_w.astype(jnp.bfloat16), "dp", scatter_dimension=0, tiled=True
        ).astype(jnp.float32),
        lax.psum_scatter(
            grad_out_w.astype(jnp.bfloat16), "dp", scatter_dimension=1, tiled=True
        ).astype(jnp.float32),
        lax.psum_scatter(
            gain_one_part.astype(jnp.bfloat16), "dp", scatter_dimension=0, tiled=True
        ).astype(jnp.float32),
    )
    gain_sums = lax.psum((attn_sums[4], mlp_sums[3]), "tensor")
    return (
        output.astype(jnp.bfloat16),
        hidden_grad,
        gain_sums[0],
        attn_sums[0],
        attn_sums[1],
        attn_sums[2],
        attn_sums[3],
        gain_sums[1],
        mlp_sums[0],
        mlp_sums[1],
        mlp_sums[2],
    )


def solution(mesh):
    in_specs = (
        P(("dp", "tensor"), None),
        P("dp"),
        P("dp"),
        P("dp", "tensor"),
        P("dp", "tensor"),
        P("dp", "tensor"),
        P("tensor", "dp"),
        P("dp"),
        P("dp", "tensor"),
        P("dp", "tensor"),
        P("tensor", "dp"),
        P(("dp", "tensor"), None),
    )
    out_specs = (
        P(("dp", "tensor"), None),
        P(("dp", "tensor"), None),
        P("dp"),
        P("dp", "tensor"),
        P("dp", "tensor"),
        P("dp", "tensor"),
        P("tensor", "dp"),
        P("dp"),
        P("dp", "tensor"),
        P("dp", "tensor"),
        P("tensor", "dp"),
    )
    return jax.shard_map(
        per_device, mesh=mesh, in_specs=in_specs, out_specs=out_specs, check_vma=False
    )
```

profile of v0, /device:TPU:0, one launch (start us, length us, event | category | flops | bytes accessed | tf_op | source)
XLA Modules:
  0.0 1160.8 jit_solution(6613281859786008414)
XLA Ops:
  12.4 23.4 %all-reduce.6 = (bf16[1536]{0:T(1024)(128)(2,1)S(1)}, bf16[1536]{0:T(1024)(128)(2,1)S(1)}) all-reduce(bf16[1536]{0:T(1024)(128)(2,1)S(1)} %dynamic-update-slice, bf16[1536]{0:T(1024)(128)(2,1)S(1)} %dynamic-update-slice.1), channel_id=1, replica_groups=mesh['dp'=8,'tensor'=4] {'dp'}, use_global_device_ids=true, to_apply=%add | all-reduce | flops 3072 | bytes 12288
  41.5 32.3 %all_gather.49 = bf16[1536,192]{1,0:T(8,128)(2,1)S(1)} all-gather(bf16[192,192]{1,0:T(8,128)(2,1)S(1)} %copy-done.29), channel_id=1, replica_groups=mesh['dp'=8,'tensor'=4] {'dp'}, dimensions={0}, use_global_device_ids=true | all-gather | bytes 663552 | tf_op jit(solution)/shard_map/all_gather | solution.py:167
  73.8 32.5 %all_gather.50 = bf16[1536,192]{1,0:T(8,128)(2,1)S(1)} all-gather(bf16[192,192]{1,0:T(8,128)(2,1)S(1)} %copy-done.30), channel_id=1, replica_groups=mesh['dp'=8,'tensor'=4] {'dp'}, dimensions={0}, use_global_device_ids=true | all-gather | bytes 663552 | tf_op jit(solution)/shard_map/all_gather | solution.py:168
  117.2 17.6 %while.27 = (s32[]{:T(128)}, bf16[2,512,2,2,96]{1,4,3,2,0:T(8,128)(2,1)S(1)}, f32[2,2,2,512]{3,2,1,0:T(2,128)S(1)}, s32[2]{0:T(128)S(1)}, s32[1024]{0:T(1024)S(1...) while((s32[]{:T(128)}, ...), condition=%wide.region_6.7_spmd, body=%wide.region_3.6_spmd.sunk | while | flops 830161408 | bytes 28948684 | solution.py:103
  135.8 17.0 %all-gather.14.cloned.1.call-done = bf16[384,1536]{0,1:T(8,128)(2,1)} async-done(((bf16[384,192]{0,1:T(8,128)(2,1)}), bf16[384,1536]{0,1:T(8,128)(2,1)}) %all-gather.14.cloned.1.call-update) | async-done | bytes 1179664 | tf_op jit(solution)/shard_map/all_gather | solution.py:169
  159.6 56.4 %reduce-scatter.12.cloned.1.call-done = f32[256,1536]{1,0:T(8,128)} async-done(((f32[1024,1536]{1,0:T(8,128)}), f32[256,1536]{1,0:T(8,128)}) %reduce-scatter.12.cloned.1.call-update) | async-done | bytes 1572880 | tf_op jit(solution)/shard_map/reduce_scatter | solution.py:197
  221.3 57.4 %all-gather.20.cloned.1.call-done = bf16[1536,1024]{1,0:T(8,128)(2,1)} async-done(((bf16[192,1024]{1,0:T(8,128)(2,1)}), bf16[1536,1024]{1,0:T(8,128)(2,1)}) %all-gather.20.cloned.1.call-update) | async-done | bytes 3145744 | tf_op jit(solution)/shard_map/all_gather | solution.py:171
  278.7 29.3 %all-gather.16.cloned.1.call-done = bf16[1024,1536]{1,0:T(8,128)(2,1)} async-done(((bf16[256,1536]{1,0:T(8,128)(2,1)}), bf16[1024,1536]{1,0:T(8,128)(2,1)}) %all-gather.16.cloned.1.call-update) | async-done | bytes 3145744 | tf_op jit(solution)/shard_map/all_gather | solution.py:201
  316.3 54.6 %all-gather.18.cloned.1.call-done = bf16[1536,1024]{1,0:T(8,128)(2,1)} async-done(((bf16[192,1024]{1,0:T(8,128)(2,1)}), bf16[1536,1024]{1,0:T(8,128)(2,1)}) %all-gather.18.cloned.1.call-update) | async-done | bytes 3145744 | tf_op jit(solution)/shard_map/all_gather | solution.py:170
  379.1 20.6 %all-gather.24.cloned.1.call-done = bf16[1024,1536]{1,0:T(8,128)(2,1)} async-done(((bf16[256,1536]{1,0:T(8,128)(2,1)}), bf16[1024,1536]{1,0:T(8,128)(2,1)}) %all-gather.24.cloned.1.call-update) | async-done | bytes 3145744 | tf_op jit(solution)/shard_map/all_gather | solution.py:227
  399.7 62.9 %all-gather.22.cloned.1.call-done = bf16[1024,1536]{0,1:T(8,128)(2,1)} async-done(((bf16[1024,192]{0,1:T(8,128)(2,1)}), bf16[1024,1536]{0,1:T(8,128)(2,1)}) %all-gather.22.cloned.1.call-update) | async-done | bytes 3145744 | tf_op jit(solution)/shard_map/all_gather | solution.py:172
  462.6 11.6 multiply_convert_fusion
  483.8 57.1 %reduce-scatter.16.cloned.1.call-done = f32[256,1536]{1,0:T(8,128)} async-done(((f32[1024,1536]{1,0:T(8,128)}), f32[256,1536]{1,0:T(8,128)}) %reduce-scatter.16.cloned.1.call-update) | async-done | bytes 1572880 | tf_op jit(solution)/shard_map/reduce_scatter | solution.py:236
  578.4 66.7 %while.28 = (s32[]{:T(128)}, f32[1024,2,96]{0,2,1:T(8,128)S(1)}, f32[1024,2,96]{0,2,1:T(8,128)}, f32[2,512,2,2,96]{1,0,4,3,2:T(2,128)}, s32[2]{0:T(128)S(1)}, /*...) while((s32[]{:T(128)}, f32[1024,2,96]{0,2,1:T(8,128)S(1)}, ...), condition=%wide.region_14.15_spmd.clone, body=%wide.region_12.14_spmd.clone.sunk | while | flops 2047474176 | bytes 74914032 | solution.py:145
  596.7 15.0 %dynamic_update_slice.20 = f32[2,512,2,2,96]{1,0,4,3,2:T(2,128)} dynamic-update-slice(f32[2,512,2,2,96]{1,0,4,3,2:T(2,128)} %get-tuple-element.405, f32[1,512,2,2,96]{1,0,4,3,2:T(1,128)S(1)} %copy.43, s32[]{:T(128)S(6)} %copy.62, s32[]{:T(128)} %constant.45.clone.1..sunk.1, s32[]{:T(128)} %constant.45.clone.1..sunk.1, s32[]{:T(128)} %constant.45.clone.1..sunk.1, s32[]{:T(128)} %constant.45.clone.1..sunk.1) | dynamic-update-slice | bytes 1572868 | tf_op jit(solution)/shard_map/while/body/jit(dynamic_update_index_in_dim)/dynamic_update_slice | solution.py:145
  630.1 15.0 %dynamic_update_slice.20 = f32[2,512,2,2,96]{1,0,4,3,2:T(2,128)} dynamic-update-slice(f32[2,512,2,2,96]{1,0,4,3,2:T(2,128)} %get-tuple-element.405, f32[1,512,2,2,96]{1,0,4,3,2:T(1,128)S(1)} %copy.43, s32[]{:T(128)S(6)} %copy.62, s32[]{:T(128)} %constant.45.clone.1..sunk.1, s32[]{:T(128)} %constant.45.clone.1..sunk.1, s32[]{:T(128)} %constant.45.clone.1..sunk.1, s32[]{:T(128)} %constant.45.clone.1..sunk.1) | dynamic-update-slice | bytes 1572868 | tf_op jit(solution)/shard_map/while/body/jit(dynamic_update_index_in_dim)/dynamic_update_slice | solution.py:145
  684.4 44.8 %reduce-scatter.30.cloned.1.call-done = bf16[192,1024]{1,0:T(8,128)(2,1)} async-done(((bf16[1536,1024]{1,0:T(8,128)(2,1)}), bf16[192,1024]{1,0:T(8,128)(2,1)}) %reduce-scatter.30.cloned.1.call-update) | async-done | bytes 393232 | tf_op jit(solution)/shard_map/reduce_scatter | solution.py:248
  731.1 75.0 %reduce-scatter.28.cloned.1.call-done = bf16[192,1024]{1,0:T(8,128)(2,1)} async-done(((bf16[1536,1024]{1,0:T(8,128)(2,1)}), bf16[192,1024]{1,0:T(8,128)(2,1)}) %reduce-scatter.28.cloned.1.call-update) | async-done | bytes 393232 | tf_op jit(solution)/shard_map/reduce_scatter | solution.py:245
  808.1 62.8 %reduce-scatter.24.cloned.1.call-done = bf16[192,192]{1,0:T(8,128)(2,1)} async-done(((bf16[1536,192]{1,0:T(8,128)(2,1)}), bf16[192,192]{1,0:T(8,128)(2,1)}) %reduce-scatter.24.cloned.1.call-update) | async-done | bytes 73744 | tf_op jit(solution)/shard_map/reduce_scatter | solution.py:294
  872.6 64.0 %reduce-scatter.22.cloned.1.call-done = bf16[192,192]{1,0:T(8,128)(2,1)} async-done(((bf16[1536,192]{1,0:T(8,128)(2,1)}), bf16[192,192]{1,0:T(8,128)(2,1)}) %reduce-scatter.22.cloned.1.call-update) | async-done | bytes 73744 | tf_op jit(solution)/shard_map/reduce_scatter | solution.py:291
  938.2 64.7 %reduce-scatter.26.cloned.1.call-done = bf16[384,192]{0,1:T(8,128)(2,1)} async-done(((bf16[384,1536]{0,1:T(8,128)(2,1)}), bf16[384,192]{0,1:T(8,128)(2,1)}) %reduce-scatter.26.cloned.1.call-update) | async-done | bytes 147472 | tf_op jit(solution)/shard_map/reduce_scatter | solution.py:297
  1004.5 64.8 %reduce-scatter.20.cloned.1.call-done = bf16[192,384]{1,0:T(8,128)(2,1)} async-done(((bf16[1536,384]{1,0:T(8,128)(2,1)}), bf16[192,384]{1,0:T(8,128)(2,1)}) %reduce-scatter.20.cloned.1.call-update) | async-done | bytes 147472 | tf_op jit(solution)/shard_map/reduce_scatter | solution.py:288
  1070.9 37.8 %reduce-scatter.18.cloned.1.call-done = bf16[256,1536]{1,0:T(8,128)(2,1)} async-done(((bf16[1024,1536]{1,0:T(8,128)(2,1)}), bf16[256,1536]{1,0:T(8,128)(2,1)}) %reduce-scatter.18.cloned.1.call-update) | async-done | bytes 786448 | tf_op jit(solution)/shard_map/reduce_scatter | solution.py:275
  1110.4 21.6 %all-reduce.5 = (bf16[1536]{0:T(1024)(128)(2,1)S(1)}, bf16[1536]{0:T(1024)(128)(2,1)S(1)}) all-reduce(bf16[1536]{0:T(1024)(128)(2,1)S(1)} %get-tuple-element.156, bf16[1536]{0:T(1024)(128)(2,1)S(1)} %copy-done.33), channel_id=6, replica_groups=mesh['dp'=8,'tensor'=4] {'dp'}, use_global_device_ids=true, to_apply=%region_18.19.clone | all-reduce | flops 3072 | bytes 12288
  (253 shorter events, 219.7 us)
Async XLA Ops:
  7.2 99.9 %all-gather.10.cloned.1.call-start = ((), (), s32[]{:S(2)}) async-start(), calls=%async_computation.11 | async-start | bytes 3932160 | tf_op jit(solution)/shard_map/all_gather | solution.py:180
  38.1 72.4 %all-gather.12.cloned.1.call-start = ((), (), s32[]{:S(2)}) async-start(), calls=%async_computation.12 | async-start | bytes 1327104 | tf_op jit(solution)/shard_map/all_gather | solution.py:166
  38.8 114.0 %all-gather.14.cloned.1.call-start = ((), (), s32[]{:S(2)}) async-start(), calls=%async_computation.13 | async-start | bytes 1327104 | tf_op jit(solution)/shard_map/all_gather | solution.py:169
  39.6 176.4 %reduce-scatter.12.cloned.1.call-start = ((), (), s32[]{:S(2)}) async-start(), calls=%async_computation.14 | async-start | bytes 7864320 | tf_op jit(solution)/shard_map/reduce_scatter | solution.py:197
  158.7 120.0 %all-gather.20.cloned.1.call-start = ((), (), s32[]{:S(2)}) async-start(), calls=%async_computation.17 | async-start | bytes 3538944 | tf_op jit(solution)/shard_map/all_gather | solution.py:171
  159.3 148.7 %all-gather.16.cloned.1.call-start = ((), (), s32[]{:S(2)}) async-start(), calls=%async_computation.15 | async-start | bytes 3932160 | tf_op jit(solution)/shard_map/all_gather | solution.py:201
  219.0 151.9 %all-gather.18.cloned.1.call-start = ((), (), s32[]{:S(2)}) async-start(), calls=%async_computation.16 | async-start | bytes 3538944 | tf_op jit(solution)/shard_map/all_gather | solution.py:170
  219.8 180.0 %all-gather.24.cloned.1.call-start = ((), (), s32[]{:S(2)}) async-start(), calls=%async_computation.20 | async-start | bytes 3932160 | tf_op jit(solution)/shard_map/all_gather | solution.py:227
  220.5 242.1 %all-gather.22.cloned.1.call-start = ((), (), s32[]{:S(2)}) async-start(), calls=%async_computation.18 | async-start | bytes 3538944 | tf_op jit(solution)/shard_map/all_gather | solution.py:172
  221.3 319.6 %reduce-scatter.16.cloned.1.call-start = ((), (), s32[]{:S(2)}) async-start(), calls=%async_computation.21 | async-start | bytes 7864320 | tf_op jit(solution)/shard_map/reduce_scatter | solution.py:236
  483.7 90.5 %all-gather.26.cloned.1.call-start = ((), (), s32[]{:S(2)}) async-start(), calls=%async_computation.22 | async-start | bytes 3932160 | tf_op jit(solution)/shard_map/all_gather | solution.py:258
  545.5 136.8 %reduce-scatter.32.cloned.1.call-start = ((), (), s32[]{:S(2)}) async-start(), calls=%async_computation.30 | async-start | bytes 3538944 | tf_op jit(solution)/shard_map/reduce_scatter | solution.py:251
  553.2 176.0 %reduce-scatter.30.cloned.1.call-start = ((), (), s32[]{:S(2)}) async-start(), calls=%async_computation.29 | async-start | bytes 3538944 | tf_op jit(solution)/shard_map/reduce_scatter | solution.py:248
  562.1 244.1 %reduce-scatter.28.cloned.1.call-start = ((), (), s32[]{:S(2)}) async-start(), calls=%async_computation.28 | async-start | bytes 3538944 | tf_op jit(solution)/shard_map/reduce_scatter | solution.py:245
  569.9 301.1 %reduce-scatter.24.cloned.1.call-start = ((), (), s32[]{:S(2)}) async-start(), calls=%async_computation.26 | async-start | bytes 884736 | tf_op jit(solution)/shard_map/reduce_scatter | solution.py:294
  650.3 286.3 %reduce-scatter.22.cloned.1.call-start = ((), (), s32[]{:S(2)}) async-start(), calls=%async_computation.25 | async-start | bytes 884736 | tf_op jit(solution)/shard_map/reduce_scatter | solution.py:291
  654.7 348.2 %reduce-scatter.26.cloned.1.call-start = ((), (), s32[]{:S(2)}) async-start(), calls=%async_computation.27 | async-start | bytes 1327104 | tf_op jit(solution)/shard_map/reduce_scatter | solution.py:297
  659.5 409.7 %reduce-scatter.20.cloned.1.call-start = ((), (), s32[]{:S(2)}) async-start(), calls=%async_computation.24 | async-start | bytes 1327104 | tf_op jit(solution)/shard_map/reduce_scatter | solution.py:288
  667.0 441.8 %reduce-scatter.18.cloned.1.call-start = ((), (), s32[]{:S(2)}) async-start(), calls=%async_computation.23 | async-start | bytes 3932160 | tf_op jit(solution)/shard_map/reduce_scatter | solution.py:275
  673.1 476.4 %reduce-scatter.14.cloned.1.call-start = ((), (), s32[]{:S(2)}) async-start(), calls=%async_computation.19 | async-start | bytes 3932160 | tf_op jit(solution)/shard_map/reduce_scatter | solution.py:209
  682.2 467.3 %copy-start.1 = (f32[256,1536]{1,0:T(8,128)S(1)}, f32[256,1536]{1,0:T(8,128)}, u32[]{:S(2)}) copy-start(f32[256,1536]{1,0:T(8,128)} %copy-done) | copy-start | bytes 4718596
  682.2 467.3 %copy-start.12 = (bf16[256,1536]{1,0:T(8,128)(2,1)S(1)}, bf16[256,1536]{1,0:T(8,128)(2,1)}, u32[]{:S(2)}) copy-start(bf16[256,1536]{1,0:T(8,128)(2,1)} %param.27) | copy-start | bytes 2359300
  682.2 467.3 %copy-start.25 = (f32[1536]{0:T(1024)S(1)}, f32[1536]{0:T(1024)}, u32[]{:S(2)}) copy-start(f32[1536]{0:T(1024)} %copy-done.24) | copy-start | bytes 18436
  682.2 467.3 %copy-start.32 = (f32[256]{0:T(256)S(1)}, f32[256]{0:T(256)}, u32[]{:S(2)}) copy-start(f32[256]{0:T(256)} %copy-done.31) | copy-start | bytes 3076
  (40 other events, 3765.0 us)
Sparse Core Ops, SparseCore 0:
  38.2 25.7 all-gather.9
  66.2 43.7 all-gather.11
  112.1 40.6 all-gather.13
  158.8 57.1 reduce-scatter.11
  218.2 60.4 all-gather.19
  280.8 27.1 all-gather.15
  310.4 60.4 all-gather.17
  372.5 27.1 all-gather.23
  402.1 60.4 all-gather.21
  483.8 56.9 reduce-scatter.15
  545.6 28.5 all-gather.25
  577.6 74.5 reduce-scatter.31
  655.7 73.3 reduce-scatter.29
  732.6 73.5 reduce-scatter.27
  809.3 61.6 reduce-scatter.23
  875.1 61.4 reduce-scatter.21
  939.8 63.0 reduce-scatter.25
  1006.1 63.1 reduce-scatter.19
  1071.8 36.9 reduce-scatter.17
  1111.3 38.1 reduce-scatter.13
where the time goes:
time: 1170 us; the launch traced here: 1160 us
  waiting for transfers between devices  788 us (67%)
  matrix products  139 us (12%)
  blocking collectives  117 us (10%)
  local copies, waits for them, and re-layouts  50.2 us (4%)
  other arithmetic  44.4 us (4%)
  between operations  17.5 us (1%)
    reduce_scatter x1, waiting for transfers between devices, per_device(): lax.psum_scatter(grad_gate_w.astype(jnp.bfloat16), 'dp', scatter_dimensio...  75 us
    reduce_scatter x1, waiting for transfers between devices, per_device(): lax.psum_scatter(grad_query_w.astype(jnp.bfloat16), 'dp', scatter_dimensi...  64.8 us
    reduce_scatter x1, waiting for transfers between devices, per_device(): lax.psum_scatter(grad_out_w.astype(jnp.bfloat16), 'dp', scatter_dimension...  64.7 us
    reduce_scatter x1, waiting for transfers between devices, per_device(): lax.psum_scatter(grad_keys_w.astype(jnp.bfloat16), 'dp', scatter_dimensio...  64 us
    all_gather x1, waiting for transfers between devices, per_device(): lax.all_gather(w_down, 'dp', axis=1, tiled=True)  62.9 us
    reduce_scatter x1, waiting for transfers between devices, per_device(): lax.psum_scatter(grad_values_w.astype(jnp.bfloat16), 'dp', scatter_dimens...  62.8 us
    all_gather x1, waiting for transfers between devices, per_device(): lax.all_gather(w_up, 'dp', axis=0, tiled=True)  57.4 us
    reduce_scatter x1, waiting for transfers between devices, per_device(): lax.psum_scatter(right_t(grad_gate, weights[4]) + right_t(grad_up, weight...  57.1 us
  transfers between devices with their start and end apart: 20, of which 17 were waited for; matrix products, arithmetic and copies ran while one was open for 16% of the time, Pallas kernels for 0%

commit v1 on v0

v1 whole, which is shorter than its diff:
```python
import math

import jax
import jax.numpy as jnp
from jax import lax
from jax.sharding import PartitionSpec as P

HD = 96
EPS = 1e-05
NEG = -1e30
THETA = 100000.0
BF = jnp.bfloat16
F32 = jnp.float32

CORE_PAIRS = [(0, 1), (1, 0), (2, 3), (3, 2)]
X_PAIRS = [(0, 2), (2, 0), (1, 3), (3, 1)]


def matmul(left_side, right_side):
    return jnp.dot(left_side, right_side, preferred_element_type=F32)


def left_t(left_side, right_side):
    return lax.dot_general(
        left_side, right_side, (((0,), (0,)), ((), ())), preferred_element_type=F32
    )


def right_t(left_side, right_side):
    return lax.dot_general(
        left_side, right_side, (((1,), (1,)), ((), ())), preferred_element_type=F32
    )


class Ring:
    def __init__(self, count):
        self.count = count
        self.half = count // 2
        order = [2 * k if k < self.half else 2 * (count - 1 - k) + 1 for k in range(count)]
        self.right = [(order[k], order[(k + 1) % count]) for k in range(count)]
        self.left = [(b, a) for a, b in self.right]
        me = lax.axis_index("dp")
        self.place = jnp.where(me % 2 == 0, me // 2, count - 1 - me // 2)

    def index(self, offset):
        place = (self.place + offset + self.count) % self.count
        return jnp.where(place < self.half, 2 * place, 2 * (self.count - 1 - place) + 1)

    def go_right(self, value):
        return lax.ppermute(value, "dp", self.right)

    def go_left(self, value):
        return lax.ppermute(value, "dp", self.left)


def cut_of(columns):
    return max(128, (columns // 2 + 127) // 128 * 128)


def gather_pieces(ring, shard):
    cut = cut_of(shard.shape[1])
    pieces = [(0, 0, shard)]
    from_left = from_right = shard
    for step in range(1, ring.half):
        from_left = ring.go_right(from_left)
        from_right = ring.go_left(from_right)
        pieces += [(-step, 0, from_left), (step, 0, from_right)]
    pieces.append((-ring.half, 0, ring.go_right(from_left[:, :cut])))
    pieces.append((ring.half, cut, ring.go_left(from_right[:, cut:])))
    return pieces


def assemble(ring, pieces):
    rows, columns = pieces[0][2].shape
    whole = jnp.zeros((ring.count * rows, columns), pieces[0][2].dtype)
    for offset, column, piece in pieces:
        whole = lax.dynamic_update_slice(whole, piece, (ring.index(offset) * rows, column))
    return whole


def scatter_sum(ring, whole):
    rows, columns = whole.shape[0] // ring.count, whole.shape[1]
    cut = cut_of(columns)

    def chunk(offset):
        return lax.dynamic_slice(whole, (ring.index(offset) * rows, 0), (rows, columns))

    far = chunk(ring.half)
    from_left = ring.go_right(far[:, :cut])
    from_right = ring.go_left(far[:, cut:])
    for step in range(ring.half - 1, 0, -1):
        to_right, to_left = chunk(step).astype(F32), chunk(-step).astype(F32)
        if step == ring.half - 1:
            to_right = jnp.concatenate(
                [to_right[:, :cut] + from_left.astype(F32), to_right[:, cut:]], axis=1
            )
            to_left = jnp.concatenate(
                [to_left[:, :cut], to_left[:, cut:] + from_right.astype(F32)], axis=1
            )
        else:
            to_right = to_right + from_left.astype(F32)
            to_left = to_left + from_right.astype(F32)
        from_left = ring.go_right(to_right.astype(BF))
        from_right = ring.go_left(to_left.astype(BF))
    return chunk(0).astype(F32) + from_left.astype(F32) + from_right.astype(F32)


def swap_core(value):
    return lax.ppermute(value, "tensor", CORE_PAIRS)


def swap_x(value):
    return lax.ppermute(value, "tensor", X_PAIRS)


def pick(pair, which):
    return lax.dynamic_index_in_dim(pair, which, 0, keepdims=False)


def in_order(own, other, which):
    return jnp.where(which == 0, jnp.stack([own, other]), jnp.stack([other, own]))


def gather_tokens(rows, core, chip):
    mine = in_order(rows, swap_core(rows), core)
    across = swap_x(rows)
    theirs = in_order(across, swap_core(across), core)
    return in_order(mine, theirs, chip)


def core_sum(partial, core):
    received = swap_core(pick(partial, 1 - core).astype(BF))
    return pick(partial, core).astype(F32) + received.astype(F32)


def sum_both(partial, core):
    chip_sum = core_sum(partial, core).astype(BF)
    return chip_sum.astype(F32) + swap_x(chip_sum).astype(F32)


def sum_own(partial, core, chip):
    away = core_sum(pick(partial, 1 - chip), core).astype(BF)
    received = swap_x(away)
    return core_sum(pick(partial, chip), core) + received.astype(F32)


def rope_tables(segment):
    places = jnp.arange(segment.shape[0], dtype=jnp.int32)
    previous = jnp.concatenate([segment[:1] - 1, segment[:-1]])
    opening = jnp.where(segment != previous, places, 0)
    position = (places - lax.cummax(opening, axis=0)).astype(F32)
    half_dim = HD // 2
    inverse = jnp.exp(-(2.0 * jnp.arange(half_dim, dtype=F32) / HD) * math.log(THETA))
    angle = position[:, None] * inverse[None, :]
    return (jnp.cos(angle), jnp.sin(angle))


def rotate(values, cosine_table, sine_table):
    half_dim = values.shape[-1] // 2
    first_half = values[..., :half_dim]
    second_half = values[..., half_dim:]
    cosine = cosine_table[:, None, :]
    sine = sine_table[:, None, :]
    return jnp.concatenate(
        [first_half * cosine - second_half * sine, second_half * cosine + first_half * sine],
        axis=-1,
    )


def unrotate(values, cosine_table, sine_table):
    return rotate(values, cosine_table, -sine_table)


def inverse_rms(values):
    return lax.rsqrt(jnp.mean(values * values, axis=-1, keepdims=True) + EPS)


def norm_back(scaled, values, inverse):
    return inverse * scaled - values * inverse * inverse * inverse * jnp.mean(
        scaled * values, axis=-1, keepdims=True
    )


def scores_of(query_rows, keys_rot, segment, offset):
    row_count = query_rows.shape[0]
    places = jnp.arange(segment.shape[0], dtype=jnp.int32)
    scores = jnp.einsum(
        "qgrd,kgd->grqk", query_rows, keys_rot, preferred_element_type=F32
    ) * HD ** (-0.5)
    row_segment = lax.dynamic_slice_in_dim(segment, offset, row_count)
    row_place = offset + jnp.arange(row_count, dtype=jnp.int32)
    allowed = (row_segment[:, None] == segment[None, :]) & (places[None, :] <= row_place[:, None])
    return jnp.where(allowed, scores, NEG)


def attend(queries, keys_rot, values, segment, block_rows):
    length = queries.shape[0]

    def one_block(block_index):
        offset = block_index * block_rows
        query_rows = lax.dynamic_slice_in_dim(queries, offset, block_rows)
        scores = scores_of(query_rows, keys_rot, segment, offset)
        log_total = jax.nn.logsumexp(scores, axis=-1)
        probs = jnp.exp(scores - log_total[..., None]).astype(BF)
        block_out = jnp.einsum("grqk,kgd->qgrd", probs, values, preferred_element_type=F32)
        return (block_out.astype(BF), log_total)

    outputs, log_totals = lax.map(one_block, jnp.arange(length // block_rows, dtype=jnp.int32))
    return (outputs.reshape(length, -1), log_totals)


def attend_back(queries, keys_rot, values, grad_heads, log_totals, segment, block_rows):
    length = queries.shape[0]
    scale = HD ** (-0.5)

    def one_block(totals, block_item):
        grad_keys, grad_values = totals
        block_index, log_total = block_item
        offset = block_index * block_rows
        query_rows = lax.dynamic_slice_in_dim(queries, offset, block_rows)
        grad_rows = lax.dynamic_slice_in_dim(grad_heads, offset, block_rows)
        scores = scores_of(query_rows, keys_rot, segment, offset)
        probs = jnp.exp(scores - log_total[..., None])
        grad_probs = jnp.einsum("qgrd,kgd->grqk", grad_rows, values, preferred_element_type=F32)
        inner_sum = jnp.sum(probs * grad_probs, axis=-1, keepdims=True)
        grad_scores = (probs * (grad_probs - inner_sum)).astype(BF)
        grad_query = (
            jnp.einsum("grqk,kgd->qgrd", grad_scores, keys_rot, preferred_element_type=F32) * scale
        )
        grad_keys = (
            grad_keys
            + jnp.einsum("grqk,qgrd->kgd", grad_scores, query_rows, preferred_element_type=F32)
            * scale
        )
        grad_values = grad_values + jnp.einsum(
            "grqk,qgrd->kgd", probs.astype(BF), grad_rows, preferred_element_type=F32
        )
        return ((grad_keys, grad_values), grad_query)

    empty_grad = jnp.zeros(keys_rot.shape, F32)
    indices = jnp.arange(length // block_rows, dtype=jnp.int32)
    (grad_keys, grad_values), grad_query = lax.scan(
        one_block, (empty_grad, empty_grad), (indices, log_totals)
    )
    return (grad_query.reshape(queries.shape), grad_keys, grad_values)


def per_device(
    dp_count,
    hidden_in,
    segments,
    attn_gain,
    w_query,
    w_key,
    w_value,
    w_out,
    mlp_gain,
    w_gate,
    w_up,
    w_down,
    cotangent,
):
    ring = Ring(dp_count)
    place = lax.axis_index("tensor")
    chip, core = place // 2, place % 2
    rows, width = hidden_in.shape
    length = segments.shape[0]
    query_columns, key_columns = w_query.shape[1], w_key.shape[1]
    query_heads, key_heads = query_columns // HD, key_columns // HD
    units = w_gate.shape[1]
    gain_one = attn_gain.astype(F32)[:, None]
    gain_two = mlp_gain.astype(F32)[:, None]

    w_qkv = jnp.concatenate([w_query, w_key, w_value], axis=1)
    w_gate_up = jnp.concatenate([w_gate, w_up], axis=1)
    shard_qkv = (w_qkv.astype(F32) * gain_one).astype(BF)
    shard_gate_up = (w_gate_up.astype(F32) * gain_two).astype(BF)
    shard_attn = jnp.concatenate([shard_qkv, w_out.T], axis=1)
    full_attn = assemble(ring, gather_pieces(ring, shard_attn))
    full_gate_up = assemble(ring, gather_pieces(ring, shard_gate_up))
    full_down = assemble(ring, gather_pieces(ring, w_down.T))
    qkv_columns = w_qkv.shape[1]
    full_qkv, full_out = full_attn[:, :qkv_columns], full_attn[:, qkv_columns:]

    hidden = gather_tokens(hidden_in, core, chip)
    grad_rows = gather_tokens(cotangent, core, chip)
    hidden_f = hidden.astype(F32)
    normed = (hidden_f * inverse_rms(hidden_f)).astype(BF).reshape(length, width)
    block_rows = min(512, length)
    cosine_table, sine_table = rope_tables(segments)
    projected = matmul(normed, full_qkv)
    queries = projected[:, :query_columns].reshape(length, query_heads, HD)
    queries = rotate(queries, cosine_table, sine_table).astype(BF)
    queries = queries.reshape(length, key_heads, query_heads // key_heads, HD)
    keys_rot = projected[:, query_columns : query_columns + key_columns]
    keys_rot = rotate(keys_rot.reshape(length, key_heads, HD), cosine_table, sine_table).astype(BF)
    values = projected[:, query_columns + key_columns :].astype(BF)
    values = values.reshape(length, key_heads, HD)
    heads_out, log_totals = attend(queries, keys_rot, values, segments, block_rows)

    branch = right_t(heads_out, full_out).reshape(2, 2, rows, width)
    resid, inverse_two, normed_two = [], [], []
    for block in range(2):
        total = sum_both(branch[block], core)
        resid.append(pick(hidden[block], core).astype(F32) + total)
        inverse_two.append(inverse_rms(resid[block]))
        part = (resid[block] * inverse_two[block]).astype(BF)
        normed_two.append(in_order(part, swap_core(part), core))
    normed_two = jnp.stack(normed_two).reshape(length, width)
    resid = jnp.stack(resid)
    inverse_two = jnp.stack(inverse_two)

    gate_up = matmul(normed_two, full_gate_up)
    gate_pre, upward = gate_up[:, :units], gate_up[:, units:]
    sigmoid_gate = jax.nn.sigmoid(gate_pre)
    silu_gate = gate_pre * sigmoid_gate
    activated = (silu_gate * upward).astype(BF)
    down = right_t(activated, full_down).reshape(2, 2, rows, width)
    output = pick(resid, chip) + sum_own(down, core, chip)

    grad_rows_flat = grad_rows.reshape(length, width)
    grad_down_w = scatter_sum(ring, left_t(grad_rows_flat, activated).astype(BF))
    grad_act = matmul(grad_rows_flat, full_down)
    grad_gate = (grad_act * upward * sigmoid_gate * (1.0 + gate_pre * (1.0 - sigmoid_gate))).astype(
        BF
    )
    grad_up = (grad_act * silu_gate).astype(BF)
    grad_gate_up = jnp.concatenate([grad_gate, grad_up], axis=1)
    grad_gate_up_w = scatter_sum(ring, left_t(normed_two, grad_gate_up).astype(BF))
    scaled_two = right_t(grad_gate_up, full_gate_up).reshape(2, 2, rows, width)
    grad_resid, grad_branch = [], []
    for block in range(2):
        total = sum_both(scaled_two[block], core)
        upstream = pick(grad_rows[block], core).astype(F32)
        grad_resid.append(upstream + norm_back(total, resid[block], inverse_two[block]))
        part = grad_resid[block].astype(BF)
        grad_branch.append(in_order(part, swap_core(part), core))
    grad_branch = jnp.stack(grad_branch).reshape(length, width)
    grad_resid = pick(jnp.stack(grad_resid), chip)

    grad_out_w = left_t(grad_branch, heads_out).astype(BF)
    grad_heads = matmul(grad_branch, full_out).astype(BF).reshape(queries.shape)
    grad_query, grad_keys, grad_values = attend_back(
        queries, keys_rot, values, grad_heads, log_totals, segments, block_rows
    )
    grad_query = unrotate(grad_query.reshape(length, query_heads, HD), cosine_table, sine_table)
    grad_keys = unrotate(grad_keys, cosine_table, sine_table)
    grad_qkv = jnp.concatenate(
        [
            grad_query.astype(BF).reshape(length, query_columns),
            grad_keys.astype(BF).reshape(length, key_columns),
            grad_values.astype(BF).reshape(length, key_columns),
        ],
        axis=1,
    )
    grad_attn_w = scatter_sum(
        ring, jnp.concatenate([left_t(normed, grad_qkv).astype(BF), grad_out_w], axis=1)
    )
    scaled_one = sum_own(right_t(grad_qkv, full_qkv).reshape(2, 2, rows, width), core, chip)
    own = hidden_in.astype(F32)
    hidden_grad = (grad_resid + norm_back(scaled_one, own, inverse_rms(own))).astype(BF)

    grad_qkv_w = grad_attn_w[:, :qkv_columns]
    gain_parts = jnp.stack(
        [
            jnp.sum(grad_qkv_w * w_qkv.astype(F32), axis=1),
            jnp.sum(grad_gate_up_w * w_gate_up.astype(F32), axis=1),
        ]
    )
    gain_sums = lax.psum(gain_parts, "tensor")
    grad_qkv_w = grad_qkv_w * gain_one
    grad_gate_up_w = grad_gate_up_w * gain_two
    return (
        output.astype(BF),
        hidden_grad,
        gain_sums[0],
        grad_qkv_w[:, :query_columns],
        grad_qkv_w[:, query_columns : query_columns + key_columns],
        grad_qkv_w[:, query_columns + key_columns :],
        grad_attn_w[:, qkv_columns:].T,
        gain_sums[1],
        grad_gate_up_w[:, :units],
        grad_gate_up_w[:, units:],
        grad_down_w.T,
    )


def solution(mesh):
    in_specs = (
        P(("dp", "tensor"), None),
        P("dp"),
        P("dp"),
        P("dp", "tensor"),
        P("dp", "tensor"),
        P("dp", "tensor"),
        P("tensor", "dp"),
        P("dp"),
        P("dp", "tensor"),
        P("dp", "tensor"),
        P("tensor", "dp"),
        P(("dp", "tensor"), None),
    )
    out_specs = (
        P(("dp", "tensor"), None),
        P(("dp", "tensor"), None),
        P("dp"),
        P("dp", "tensor"),
        P("dp", "tensor"),
        P("dp", "tensor"),
        P("tensor", "dp"),
        P("dp"),
        P("dp", "tensor"),
        P("dp", "tensor"),
        P("tensor", "dp"),
    )
    dp_count = mesh.shape["dp"]

    def body(*arrays):
        return per_device(dp_count, *arrays)

    return jax.shard_map(body, mesh=mesh, in_specs=in_specs, out_specs=out_specs, check_vma=False)
```

time: 1170 us -> 520 us (0.44)
  waiting for transfers between devices: 788 us -> 170 us
  blocking collectives: 117 us -> 5.84 us
  starting transfers between devices: 1.66 us -> 66.7 us
  local copies, waits for them, and re-layouts: 50.2 us -> 93.5 us
  matrix products: 139 us -> 106 us
  between operations: 17.5 us -> 2.55 us
    reduce_scatter x11 -> x0, waiting for transfers between devices: 538 us -> none  [the longest x1 75 us: per_device(): lax.psum_scatter(grad_gate_w.astype(jnp.bfloat16), 'dp', scatter_dimensio...]
    all_gather x9 -> x0, waiting for transfers between devices: 246 us -> none  [the longest x1 62.9 us: per_device(): lax.all_gather(w_down, 'dp', axis=1, tiled=True)]
    ppermute x0 -> x72, waiting for transfers between devices: none -> 170 us  [the longest x24 86.2 us: go_right(): return lax.ppermute(value, 'dp', self.right)]
    ppermute x0 -> x72, starting transfers between devices: none -> 66.7 us  [the longest x24 35.5 us: go_right(): return lax.ppermute(value, 'dp', self.right)]
    all_gather x2 -> x0, blocking collectives: 64.8 us -> none  [the longest x1 32.5 us: per_device(): lax.all_gather(w_value, 'dp', axis=0, tiled=True)]
    unnamed x2 -> x0, blocking collectives: 45 us -> none
    dynamic_update_slice x0 -> x24, local copies, waits for them, and re-layouts: none -> 28.6 us  [assemble(): lax.dynamic_update_slice(whole, piece, (ring.index(offset) * rows, column))]
    dot_general x7 -> x4, matrix products: 37.6 us -> 20 us  [left_t(): lax.dot_general(left_side, right_side, (((0,), (0,)), ((), ())), preferre...]
  transfers between devices with their start and end apart: 20 -> 72, of which waited for: 17 -> 33; matrix products, arithmetic and copies ran while one was open for 16% -> 37% of each run, Pallas kernels for 0% -> 0%
where the time goes in v1:
time: 520 us; the launch traced here: 513 us
  waiting for transfers between devices  170 us (33%)
  matrix products  106 us (20%)
  local copies, waits for them, and re-layouts  93.5 us (18%)
  starting transfers between devices  66.7 us (13%)
  other arithmetic  55.9 us (11%)
  loops' own time  12.6 us (2%)
  blocking collectives  5.84 us (1%)
    ppermute x24, waiting for transfers between devices, go_right(): return lax.ppermute(value, 'dp', self.right)  86.2 us
    ppermute x24, waiting for transfers between devices, go_left(): return lax.ppermute(value, 'dp', self.left)  59.3 us
    ppermute x24, starting transfers between devices, go_right(): return lax.ppermute(value, 'dp', self.right)  35.5 us
    dynamic_update_slice x4, local copies, waits for them, and re-layouts, attend_back(): lax.scan(one_block, (empty_grad, empty_grad), (indices, log_totals))  31.4 us
    dynamic_update_slice x24, local copies, waits for them, and re-layouts, assemble(): lax.dynamic_update_slice(whole, piece, (ring.index(offset) * rows, column))  28.6 us
    dot_general x4, matrix products, matmul(): return jnp.dot(left_side, right_side, preferred_element_type=F32)  28.2 us
    dot_general x4, matrix products, right_t(): lax.dot_general(left_side, right_side, (((1,), (1,)), ((), ())), preferre...  23.9 us
    ppermute x8, waiting for transfers between devices, swap_x(): return lax.ppermute(value, 'tensor', X_PAIRS)  22.1 us
  transfers between devices with their start and end apart: 72, of which 33 were waited for; matrix products, arithmetic and copies ran while one was open for 37% of the time, Pallas kernels for 0%

profile of v1, /device:TPU:0, one launch (start us, length us, event | category | flops | bytes accessed | tf_op | source)
XLA Modules:
  0.0 512.9 jit_solution(15206223433615483574)
XLA Ops:
  36.8 7.4 %collective-permute-done.17 = bf16[192,2048]{1,0:T(8,128)(2,1)} collective-permute-done((bf16[192,2048]{1,0:T(8,128)(2,1)S(1)}, bf16[192,2048]{1,0:T(8,128)(2,1)}, u32[]{:S(2)}, u32[]{:S(2)}) %collective-permute-start.17) | collective-permute-done | bytes 786464 | tf_op jit(solution)/shard_map/ppermute | solution.py:50
  87.5 12.7 %collective-permute-done.31 = bf16[192,512]{1,0:T(8,128)(2,1)S(1)} collective-permute-done((bf16[192,512]{1,0:T(8,128)(2,1)S(1)}, bf16[192,512]{1,0:T(8,128)(2,1)S(1)}, u32[]{:S(2)}, u32[]{:S(2)}) %collective-permute-start.31) | collective-permute-done | bytes 196640 | tf_op jit(solution)/shard_map/ppermute | solution.py:50
  115.8 30.2 %while.27 = (s32[]{:T(128)}, bf16[2,512,2,2,96]{1,4,3,2,0:T(8,128)(2,1)}, f32[2,2,2,512]{3,2,1,0:T(2,128)}, s32[2]{0:T(128)S(1)}, s32[1024]{0:T(1024)S(1)}, /*in...) while((s32[]{:T(128)}, ...), condition=%wide.region_6.7_spmd, body=%wide.region_3.6_spmd.sunk | while | flops 830161408 | bytes 35240196 | solution.py:208
  166.0 10.9 %collective-permute-done.21 = bf16[192,2048]{1,0:T(8,128)(2,1)S(1)} collective-permute-done((bf16[192,2048]{1,0:T(8,128)(2,1)}, bf16[192,2048]{1,0:T(8,128)(2,1)S(1)}, u32[]{:S(2)}, u32[]{:S(2)}) %collective-permute-start.21) | collective-permute-done | bytes 786464 | tf_op jit(solution)/shard_map/ppermute | solution.py:50
  193.3 6.9 %collective-permute-done.12 = bf16[256,1536]{1,0:T(8,128)(2,1)S(1)} collective-permute-done((bf16[256,1536]{1,0:T(8,128)(2,1)S(1)}, bf16[256,1536]{1,0:T(8,128)(2,1)S(1)}, u32[]{:S(2)}, u32[]{:S(2)}) %collective-permute-start.12) | collective-permute-done | bytes 786464 | tf_op jit(solution)/shard_map/ppermute | solution.py:113
  203.8 11.9 %fusion.130 = f32[1024,2048]{1,0:T(8,128)} fusion(bf16[1024,1536]{1,0:T(8,128)(2,1)S(1)} %bitcast.353, bf16[1536,2048]{1,0:T(8,128)(2,1)} %constant_dynamic-update-slice_fusion.25), kind=kOutput, calls=%fused_computation.305 | convolution fusion | flops 6442450944 | bytes 17825792 | tf_op jit(solution)/shard_map/dot_general | solution.py:20
  215.7 9.1 %multiply_convert_fusion.1 = (bf16[1024,1024]{1,0:T(8,128)(2,1)S(1)}, bf16[1024,1024]{1,0:T(8,128)(2,1)S(1)}, bf16[1024,1024]{1,0:T(8,128)(2,1)}) fusion(f32[1024,2048]{1,0:T(8,128)} %fusion.130, bf16[1024,1536]{1,0:T(8,128)(2,1)S(1)} %bitcast.329, bf16[1536,1024]{1,0:T(8,128)(2,1)} %get-tuple-element.304), kind=kOutput, calls=%fused_computation.88 | convolution fusion | flops 3236954112 | bytes 20971520 | tf_op jit(solution)/shard_map/dot_general | solution.py:20
  226.1 8.8 %fusion.63 = f32[1024,1536]{1,0:T(8,128)S(1)} fusion(bf16[1536,2048]{1,0:T(8,128)(2,1)} %constant_dynamic-update-slice_fusion.25, bf16[1024,1024]{1,0:T(8,128)(2,1)S(1)} %get-tuple-element.244, bf16[1024,1024]{1,0:T(8,128)(2,1)S(1)} %get-tuple-element.243), kind=kOutput, calls=%fused_computation.103 | convolution fusion | flops 6450839552 | bytes 16777216 | tf_op jit(solution)/shard_map/dot_general | solution.py:30
  234.9 9.1 %convolution_convert_fusion = bf16[1536,2048]{1,0:T(8,128)(2,1)S(1)} fusion(bf16[1024,1536]{1,0:T(8,128)(2,1)} %bitcast.354, bf16[1024,1024]{1,0:T(8,128)(2,1)} %copy-done.38, bf16[1024,1024]{1,0:T(8,128)(2,1)S(1)} %get-tuple-element.243), kind=kOutput, calls=%fused_computation.74 | convolution fusion | flops 6453985280 | bytes 13631488 | tf_op jit(solution)/shard_map/dot_general | solution.py:24
  249.1 7.6 %fusion.131 = f32[1024,1536]{1,0:T(8,128)} fusion(bf16[1024,1024]{1,0:T(8,128)(2,1)S(1)} %copy-done.39, bf16[1536,1024]{1,0:T(8,128)(2,1)} %get-tuple-element.304), kind=kOutput, calls=%fused_computation.306 | convolution fusion | flops 3221225472 | bytes 11534336 | tf_op jit(solution)/shard_map/dot_general | solution.py:30
  267.4 6.8 %collective-permute-done.56 = bf16[192,1024]{1,0:T(8,128)(2,1)S(1)} collective-permute-done((bf16[192,1024]{1,0:T(8,128)(2,1)S(1)}, bf16[192,1024]{1,0:T(8,128)(2,1)S(1)}, u32[]{:S(2)}, u32[]{:S(2)}) %collective-permute-start.56) | collective-permute-done | bytes 393248 | tf_op jit(solution)/shard_map/ppermute | solution.py:50
  278.2 7.5 %collective-permute-done.65 = bf16[192,1024]{1,0:T(8,128)(2,1)S(1)} collective-permute-done((bf16[192,1024]{1,0:T(8,128)(2,1)S(1)}, bf16[192,1024]{1,0:T(8,128)(2,1)S(1)}, u32[]{:S(2)}, u32[]{:S(2)}) %collective-permute-start.65) | collective-permute-done | bytes 393248 | tf_op jit(solution)/shard_map/ppermute | solution.py:50
  290.7 7.0 %collective-permute-done.69 = bf16[192,1024]{1,0:T(8,128)(2,1)S(1)} collective-permute-done((bf16[192,1024]{1,0:T(8,128)(2,1)S(1)}, bf16[192,1024]{1,0:T(8,128)(2,1)S(1)}, u32[]{:S(2)}, u32[]{:S(2)}) %collective-permute-start.69) | collective-permute-done | bytes 393248 | tf_op jit(solution)/shard_map/ppermute | solution.py:53
  298.2 14.7 %collective-permute-done.66 = bf16[192,1024]{1,0:T(8,128)(2,1)S(1)} collective-permute-done((bf16[192,1024]{1,0:T(8,128)(2,1)S(1)}, bf16[192,1024]{1,0:T(8,128)(2,1)S(1)}, u32[]{:S(2)}, u32[]{:S(2)}) %collective-permute-start.66) | collective-permute-done | bytes 393248 | tf_op jit(solution)/shard_map/ppermute | solution.py:50
  316.7 5.8 %collective-permute-done.70 = bf16[192,1024]{1,0:T(8,128)(2,1)S(1)} collective-permute-done((bf16[192,1024]{1,0:T(8,128)(2,1)S(1)}, bf16[192,1024]{1,0:T(8,128)(2,1)S(1)}, u32[]{:S(2)}, u32[]{:S(2)}) %collective-permute-start.70) | collective-permute-done | bytes 393248 | tf_op jit(solution)/shard_map/ppermute | solution.py:53
  324.2 9.1 %collective-permute-done.40 = bf16[256,1536]{1,0:T(8,128)(2,1)S(1)} collective-permute-done((bf16[256,1536]{1,0:T(8,128)(2,1)S(1)}, bf16[256,1536]{1,0:T(8,128)(2,1)S(1)}, u32[]{:S(2)}, u32[]{:S(2)}) %collective-permute-start.40) | collective-permute-done | bytes 786464 | tf_op jit(solution)/shard_map/ppermute | solution.py:113
  339.4 6.0 %collective-permute-done.35 = bf16[256,1536]{1,0:T(8,128)(2,1)S(1)} collective-permute-done((bf16[256,1536]{1,0:T(8,128)(2,1)S(1)}, bf16[256,1536]{1,0:T(8,128)(2,1)S(1)}, u32[]{:S(2)}, u32[]{:S(2)}) %collective-permute-start.35) | collective-permute-done | bytes 786464 | tf_op jit(solution)/shard_map/ppermute | solution.py:113
  359.0 65.7 %while.28 = (s32[]{:T(128)}, f32[1024,2,96]{0,2,1:T(8,128)S(1)}, f32[1024,2,96]{0,2,1:T(8,128)}, f32[2,512,2,2,96]{1,0,4,3,2:T(2,128)}, s32[2]{0:T(128)S(1)}, /*...) while((s32[]{:T(128)}, f32[1024,2,96]{0,2,1:T(8,128)S(1)}, ...), condition=%wide.region_14.15_spmd.clone, body=%wide.region_12.14_spmd.clone.sunk | while | flops 2047474176 | bytes 74914032 | solution.py:242
  376.6 14.9 %dynamic_update_slice.155 = f32[2,512,2,2,96]{1,0,4,3,2:T(2,128)} dynamic-update-slice(f32[2,512,2,2,96]{1,0,4,3,2:T(2,128)} %get-tuple-element.484, f32[1,512,2,2,96]{1,0,4,3,2:T(1,128)S(1)} %copy.108, s32[]{:T(128)S(6)} %copy.152, s32[]{:T(128)} %constant.488.clone.1..sunk.1, s32[]{:T(128)} %constant.488.clone.1..sunk.1, s32[]{:T(128)} %constant.488.clone.1..sunk.1, s32[]{:T(128)} %constant.488.clone.1..sunk.1) | dynamic-update-slice | bytes 1572868 | tf_op jit(solution)/shard_map/while/body/jit(dynamic_update_index_in_dim)/dynamic_update_slice | solution.py:242
  409.8 14.9 %dynamic_update_slice.155 = f32[2,512,2,2,96]{1,0,4,3,2:T(2,128)} dynamic-update-slice(f32[2,512,2,2,96]{1,0,4,3,2:T(2,128)} %get-tuple-element.484, f32[1,512,2,2,96]{1,0,4,3,2:T(1,128)S(1)} %copy.108, s32[]{:T(128)S(6)} %copy.152, s32[]{:T(128)} %constant.488.clone.1..sunk.1, s32[]{:T(128)} %constant.488.clone.1..sunk.1, s32[]{:T(128)} %constant.488.clone.1..sunk.1, s32[]{:T(128)} %constant.488.clone.1..sunk.1) | dynamic-update-slice | bytes 1572868 | tf_op jit(solution)/shard_map/while/body/jit(dynamic_update_index_in_dim)/dynamic_update_slice | solution.py:242
  450.2 6.5 %collective-permute-done.53 = bf16[192,1152]{1,0:T(8,128)(2,1)S(1)} collective-permute-done((bf16[192,1152]{1,0:T(8,128)(2,1)S(1)}, bf16[192,1152]{1,0:T(8,128)(2,1)S(1)}, u32[]{:S(2)}, u32[]{:S(2)}) %collective-permute-start.53) | collective-permute-done | bytes 442400 | tf_op jit(solution)/shard_map/ppermute | solution.py:53
  461.7 6.5 %collective-permute-done.50 = bf16[192,1152]{1,0:T(8,128)(2,1)S(1)} collective-permute-done((bf16[192,1152]{1,0:T(8,128)(2,1)S(1)}, bf16[192,1152]{1,0:T(8,128)(2,1)S(1)}, u32[]{:S(2)}, u32[]{:S(2)}) %collective-permute-start.50) | collective-permute-done | bytes 442400 | tf_op jit(solution)/shard_map/ppermute | solution.py:50
  469.7 13.3 %collective-permute-done.54 = bf16[192,1152]{1,0:T(8,128)(2,1)S(1)} collective-permute-done((bf16[192,1152]{1,0:T(8,128)(2,1)S(1)}, bf16[192,1152]{1,0:T(8,128)(2,1)S(1)}, u32[]{:S(2)}, u32[]{:S(2)}) %collective-permute-start.54) | collective-permute-done | bytes 442400 | tf_op jit(solution)/shard_map/ppermute | solution.py:53
  497.5 5.8 %psum.7 = f32[2,192]{1,0:T(2,128)S(1)} all-reduce(f32[2,192]{1,0:T(2,128)S(1)} %pad_maximum_fusion.21), channel_id=1, replica_groups=mesh['dp'=8,'tensor'=4] {'tensor'}, use_global_device_ids=true, to_apply=%region_18.19 | all-reduce | flops 384 | bytes 3072 | tf_op jit(solution)/shard_map/psum | solution.py:370
  (419 shorter events, 294.4 us)
Async XLA Ops:
  21.3 26.9 %collective-permute-start = (bf16[256,1536]{1,0:T(8,128)(2,1)S(1)}, bf16[256,1536]{1,0:T(8,128)(2,1)S(1)}, u32[]{:S(2)}, u32[]{:S(2)}) collective-permute-start(bf16[256,1536]{1,0:T(8,128)(2,1)S(1)} %copy-done.4), channel_id=1, source_target_pairs={{0,1},{1,0},{2,3},{3,2},{4,5},{5,4},{6,7},{7,6},{8,9},{9,8},{10,11... | collective-permute-start | bytes 2359304 | tf_op jit(solution)/shard_map/ppermute | solution.py:109
  27.4 43.1 %collective-permute-start.1 = (bf16[256,1536]{1,0:T(8,128)(2,1)S(1)}, bf16[256,1536]{1,0:T(8,128)(2,1)S(1)}, u32[]{:S(2)}, u32[]{:S(2)}) collective-permute-start(bf16[256,1536]{1,0:T(8,128)(2,1)S(1)} %copy-done.4), channel_id=1, source_target_pairs={{0,2},{2,0},{1,3},{3,1},{4,6},{6,4},{5,7},{7,5},{8,10},{10,8},{9,1... | collective-permute-start | bytes 2359304 | tf_op jit(solution)/shard_map/ppermute | solution.py:113
  30.7 31.4 %collective-permute-start.18 = (bf16[192,2048]{1,0:T(8,128)(2,1)S(1)}, bf16[192,2048]{1,0:T(8,128)(2,1)}, u32[]{:S(2)}, u32[]{:S(2)}) collective-permute-start(bf16[192,2048]{1,0:T(8,128)(2,1)S(1)} %get-tuple-element.232), channel_id=1, source_target_pairs={{8,0},{16,8},{24,16},{28,24},{20,28},{12,20},{4,12},{0,4},{9,1},{1... | collective-permute-start | bytes 2359304 | tf_op jit(solution)/shard_map/ppermute | solution.py:53
  70.4 35.7 %collective-permute-start.37 = (bf16[256,1536]{1,0:T(8,128)(2,1)S(1)}, bf16[256,1536]{1,0:T(8,128)(2,1)}, u32[]{:S(2)}, u32[]{:S(2)}) collective-permute-start(bf16[256,1536]{1,0:T(8,128)(2,1)S(1)} %copy-done.26), channel_id=1, source_target_pairs={{0,2},{2,0},{1,3},{3,1},{4,6},{6,4},{5,7},{7,5},{8,10},{10,8},{9,1... | collective-permute-start | bytes 2359304 | tf_op jit(solution)/shard_map/ppermute | solution.py:113
  71.7 31.0 %collective-permute-start.2 = (bf16[256,1536]{1,0:T(8,128)(2,1)S(1)}, bf16[256,1536]{1,0:T(8,128)(2,1)S(1)}, u32[]{:S(2)}, u32[]{:S(2)}) collective-permute-start(bf16[256,1536]{1,0:T(8,128)(2,1)S(1)} %collective-permute-done.1), channel_id=1, source_target_pairs={{0,1},{1,0},{2,3},{3,2},{4,5},{5,4},{6,7},{7,6},{8,9},{9,8},{10,11... | collective-permute-start | bytes 2359304 | tf_op jit(solution)/shard_map/ppermute | solution.py:109
  77.5 79.0 %collective-permute-start.19 = (bf16[192,2048]{1,0:T(8,128)(2,1)}, bf16[192,2048]{1,0:T(8,128)(2,1)}, u32[]{:S(2)}, u32[]{:S(2)}) collective-permute-start(bf16[192,2048]{1,0:T(8,128)(2,1)} %collective-permute-done.17), channel_id=1, source_target_pairs={{0,8},{8,16},{16,24},{24,28},{28,20},{20,12},{12,4},{4,0},{1,9},{9... | collective-permute-start | bytes 2359304 | tf_op jit(solution)/shard_map/ppermute | solution.py:50
  106.2 55.2 %collective-permute-start.20 = (bf16[192,2048]{1,0:T(8,128)(2,1)}, bf16[192,2048]{1,0:T(8,128)(2,1)}, u32[]{:S(2)}, u32[]{:S(2)}) collective-permute-start(bf16[192,2048]{1,0:T(8,128)(2,1)} %collective-permute-done.18), channel_id=1, source_target_pairs={{8,0},{16,8},{24,16},{28,24},{20,28},{12,20},{4,12},{0,4},{9,1},{1... | collective-permute-start | bytes 2359304 | tf_op jit(solution)/shard_map/ppermute | solution.py:53
  107.9 45.4 %collective-permute-start.38 = (bf16[256,1536]{1,0:T(8,128)(2,1)}, bf16[256,1536]{1,0:T(8,128)(2,1)}, u32[]{:S(2)}, u32[]{:S(2)}) collective-permute-start(bf16[256,1536]{1,0:T(8,128)(2,1)} %collective-permute-done.37), channel_id=1, source_target_pairs={{0,1},{1,0},{2,3},{3,2},{4,5},{5,4},{6,7},{7,6},{8,9},{9,8},{10,11... | collective-permute-start | bytes 2359304 | tf_op jit(solution)/shard_map/ppermute | solution.py:109
  163.7 28.7 %collective-permute-start.14 = (bf16[256,1536]{1,0:T(8,128)(2,1)S(1)}, bf16[256,1536]{1,0:T(8,128)(2,1)S(1)}, u32[]{:S(2)}, u32[]{:S(2)}) collective-permute-start(bf16[256,1536]{1,0:T(8,128)(2,1)S(1)} %fusion.90), channel_id=1, source_target_pairs={{0,2},{2,0},{1,3},{3,1},{4,6},{6,4},{5,7},{7,5},{8,10},{10,8},{9,1... | collective-permute-start | bytes 2359304 | tf_op jit(solution)/shard_map/ppermute | solution.py:113
  164.8 35.4 %collective-permute-start.12 = (bf16[256,1536]{1,0:T(8,128)(2,1)S(1)}, bf16[256,1536]{1,0:T(8,128)(2,1)S(1)}, u32[]{:S(2)}, u32[]{:S(2)}) collective-permute-start(bf16[256,1536]{1,0:T(8,128)(2,1)S(1)} %fusion.91), channel_id=1, source_target_pairs={{0,2},{2,0},{1,3},{3,1},{4,6},{6,4},{5,7},{7,5},{8,10},{10,8},{9,1... | collective-permute-start | bytes 2359304 | tf_op jit(solution)/shard_map/ppermute | solution.py:113
  260.8 25.2 %collective-permute-start.41 = (bf16[256,1536]{1,0:T(8,128)(2,1)S(1)}, bf16[256,1536]{1,0:T(8,128)(2,1)S(1)}, u32[]{:S(2)}, u32[]{:S(2)}) collective-permute-start(bf16[256,1536]{1,0:T(8,128)(2,1)S(1)} %fusion.101), channel_id=1, source_target_pairs={{0,1},{1,0},{2,3},{3,2},{4,5},{5,4},{6,7},{7,6},{8,9},{9,8},{10,11... | collective-permute-start | bytes 2359304 | tf_op jit(solution)/shard_map/ppermute | solution.py:109
  260.8 27.0 %collective-permute-start.39 = (bf16[256,1536]{1,0:T(8,128)(2,1)S(1)}, bf16[256,1536]{1,0:T(8,128)(2,1)S(1)}, u32[]{:S(2)}, u32[]{:S(2)}) collective-permute-start(bf16[256,1536]{1,0:T(8,128)(2,1)S(1)} %fusion.100), channel_id=1, source_target_pairs={{0,1},{1,0},{2,3},{3,2},{4,5},{5,4},{6,7},{7,6},{8,9},{9,8},{10,11... | collective-permute-start | bytes 2359304 | tf_op jit(solution)/shard_map/ppermute | solution.py:109
  267.2 70.8 %collective-permute-start.33 = (bf16[256,1536]{1,0:T(8,128)(2,1)S(1)}, bf16[256,1536]{1,0:T(8,128)(2,1)S(1)}, u32[]{:S(2)}, u32[]{:S(2)}) collective-permute-start(bf16[256,1536]{1,0:T(8,128)(2,1)S(1)} %get-tuple-element.260), channel_id=1, source_target_pairs={{0,1},{1,0},{2,3},{3,2},{4,5},{5,4},{6,7},{7,6},{8,9},{9,8},{10,11... | collective-permute-start | bytes 2359304 | tf_op jit(solution)/shard_map/ppermute | solution.py:109
  286.0 62.6 %collective-permute-start.61 = (bf16[192,2048]{1,0:T(8,128)(2,1)S(1)}, bf16[192,2048]{1,0:T(8,128)(2,1)S(1)}, u32[]{:S(2)}, u32[]{:S(2)}) collective-permute-start(bf16[192,2048]{1,0:T(8,128)(2,1)S(1)} %pad_maximum_fusion.10), channel_id=1, source_target_pairs={{8,0},{16,8},{24,16},{28,24},{20,28},{12,20},{4,12},{0,4},{9,1},{1... | collective-permute-start | bytes 2359304 | tf_op jit(solution)/shard_map/ppermute | solution.py:53
  287.8 26.8 %collective-permute-start.57 = (bf16[192,2048]{1,0:T(8,128)(2,1)S(1)}, bf16[192,2048]{1,0:T(8,128)(2,1)S(1)}, u32[]{:S(2)}, u32[]{:S(2)}) collective-permute-start(bf16[192,2048]{1,0:T(8,128)(2,1)S(1)} %pad_maximum_fusion.9), channel_id=1, source_target_pairs={{0,8},{8,16},{16,24},{24,28},{28,20},{20,12},{12,4},{4,0},{1,9},{9... | collective-permute-start | bytes 2359304 | tf_op jit(solution)/shard_map/ppermute | solution.py:50
  288.6 24.3 %collective-permute-start.66 = (bf16[192,1024]{1,0:T(8,128)(2,1)S(1)}, bf16[192,1024]{1,0:T(8,128)(2,1)S(1)}, u32[]{:S(2)}, u32[]{:S(2)}) collective-permute-start(bf16[192,1024]{1,0:T(8,128)(2,1)S(1)} %add_convert_fusion.11), channel_id=1, source_target_pairs={{0,8},{8,16},{16,24},{24,28},{28,20},{20,12},{12,4},{4,0},{1,9},{9... | collective-permute-start | bytes 1179656 | tf_op jit(solution)/shard_map/ppermute | solution.py:50
  297.7 25.5 %collective-permute-start.42 = (bf16[256,1536]{1,0:T(8,128)(2,1)S(1)}, bf16[256,1536]{1,0:T(8,128)(2,1)S(1)}, u32[]{:S(2)}, u32[]{:S(2)}) collective-permute-start(bf16[256,1536]{1,0:T(8,128)(2,1)S(1)} %fusion.86), channel_id=1, source_target_pairs={{0,2},{2,0},{1,3},{3,1},{4,6},{6,4},{5,7},{7,5},{8,10},{10,8},{9,1... | collective-permute-start | bytes 2359304 | tf_op jit(solution)/shard_map/ppermute | solution.py:113
  323.2 23.8 %collective-permute-start.67 = (bf16[192,1024]{1,0:T(8,128)(2,1)S(1)}, bf16[192,1024]{1,0:T(8,128)(2,1)S(1)}, u32[]{:S(2)}, u32[]{:S(2)}) collective-permute-start(bf16[192,1024]{1,0:T(8,128)(2,1)S(1)} %get-tuple-element.271), channel_id=1, source_target_pairs={{0,8},{8,16},{16,24},{24,28},{28,20},{20,12},{12,4},{4,0},{1,9},{9... | collective-permute-start | bytes 1179656 | tf_op jit(solution)/shard_map/ppermute | solution.py:50
  350.4 134.5 %collective-permute-start.59 = (bf16[192,2048]{1,0:T(8,128)(2,1)}, bf16[192,2048]{1,0:T(8,128)(2,1)}, u32[]{:S(2)}, u32[]{:S(2)}) collective-permute-start(bf16[192,2048]{1,0:T(8,128)(2,1)} %get-tuple-element.248), channel_id=1, source_target_pairs={{0,8},{8,16},{16,24},{24,28},{28,20},{20,12},{12,4},{4,0},{1,9},{9... | collective-permute-start | bytes 2359304 | tf_op jit(solution)/shard_map/ppermute | solution.py:50
  351.1 96.4 %collective-permute-start.62 = (bf16[192,2048]{1,0:T(8,128)(2,1)}, bf16[192,2048]{1,0:T(8,128)(2,1)}, u32[]{:S(2)}, u32[]{:S(2)}) collective-permute-start(bf16[192,2048]{1,0:T(8,128)(2,1)} %get-tuple-element.249), channel_id=1, source_target_pairs={{8,0},{16,8},{24,16},{28,24},{20,28},{12,20},{4,12},{0,4},{9,1},{1... | collective-permute-start | bytes 2359304 | tf_op jit(solution)/shard_map/ppermute | solution.py:53
  440.8 65.7 %collective-permute-start.45 = (bf16[256,1536]{1,0:T(8,128)(2,1)}, bf16[256,1536]{1,0:T(8,128)(2,1)}, u32[]{:S(2)}, u32[]{:S(2)}) collective-permute-start(bf16[256,1536]{1,0:T(8,128)(2,1)} %get-tuple-element.256), channel_id=1, source_target_pairs={{0,1},{1,0},{2,3},{3,2},{4,5},{5,4},{6,7},{7,6},{8,9},{9,8},{10,11... | collective-permute-start | bytes 2359304 | tf_op jit(solution)/shard_map/ppermute | solution.py:109
  456.7 28.7 %collective-permute-start.63 = (bf16[192,2048]{1,0:T(8,128)(2,1)S(1)}, bf16[192,2048]{1,0:T(8,128)(2,1)S(1)}, u32[]{:S(2)}, u32[]{:S(2)}) collective-permute-start(bf16[192,2048]{1,0:T(8,128)(2,1)S(1)} %add_convert_fusion), channel_id=1, source_target_pairs={{8,0},{16,8},{24,16},{28,24},{20,28},{12,20},{4,12},{0,4},{9,1},{1... | collective-permute-start | bytes 2359304 | tf_op jit(solution)/shard_map/ppermute | solution.py:53
  459.1 24.0 %collective-permute-start.54 = (bf16[192,1152]{1,0:T(8,128)(2,1)S(1)}, bf16[192,1152]{1,0:T(8,128)(2,1)S(1)}, u32[]{:S(2)}, u32[]{:S(2)}) collective-permute-start(bf16[192,1152]{1,0:T(8,128)(2,1)S(1)} %get-tuple-element.267), channel_id=1, source_target_pairs={{8,0},{16,8},{24,16},{28,24},{20,28},{12,20},{4,12},{0,4},{9,1},{1... | collective-permute-start | bytes 1327112 | tf_op jit(solution)/shard_map/ppermute | solution.py:53
  468.3 38.2 %collective-permute-start.47 = (bf16[256,1536]{1,0:T(8,128)(2,1)}, bf16[256,1536]{1,0:T(8,128)(2,1)}, u32[]{:S(2)}, u32[]{:S(2)}) collective-permute-start(bf16[256,1536]{1,0:T(8,128)(2,1)} %fusion.84), channel_id=1, source_target_pairs={{0,2},{2,0},{1,3},{3,1},{4,6},{6,4},{5,7},{7,5},{8,10},{10,8},{9,1... | collective-permute-start | bytes 2359304 | tf_op jit(solution)/shard_map/ppermute | solution.py:113
  (90 other events, 1155.2 us)

commit v2 on v1

v2 whole, which is shorter than its diff:
```python
import functools
import math

import jax
import jax.numpy as jnp
from jax import lax
from jax.experimental import pallas as pl
from jax.experimental.pallas import tpu as pltpu
from jax.sharding import PartitionSpec as P

HD = 96
HALF = HD // 2
EPS = 1e-05
NEG = -1e30
THETA = 100000.0
SCALE = HD ** (-0.5)
LOG2E = math.log2(math.e)
BF = jnp.bfloat16
F32 = jnp.float32
MIB = 1024 * 1024

CORE_PAIRS = [(0, 1), (1, 0), (2, 3), (3, 2)]
X_PAIRS = [(0, 2), (2, 0), (1, 3), (3, 1)]


def dot(left_side, right_side):
    return jnp.dot(left_side, right_side, preferred_element_type=F32)


def dot_nt(left_side, right_side):
    return lax.dot_general(
        left_side, right_side, (((1,), (1,)), ((), ())), preferred_element_type=F32
    )


def turned(value):
    return value.astype(F32).T


def after(value, *others):
    return lax.optimization_barrier((value, *others))[0]


def params(mib):
    return pltpu.CompilerParams(vmem_limit_bytes=mib * MIB)


def cost(flops, size, exps=0):
    return pl.CostEstimate(flops=flops, bytes_accessed=size, transcendentals=exps)


ANY = pl.BlockSpec(memory_space=pl.ANY)
SMEM = pl.BlockSpec(memory_space=pltpu.SMEM)
VMEM = pl.BlockSpec(memory_space=pltpu.VMEM)


def assemble_kernel(spans, place_ref, *refs):
    pieces, whole, sems = refs[: len(spans)], refs[len(spans)], refs[len(spans) + 1]
    copies = []
    for k, (column, width) in enumerate(spans):
        rows = pieces[k].shape[0]
        at = pl.multiple_of(place_ref[k], 16)
        copies.append(
            pltpu.make_async_copy(
                pieces[k], whole.at[pl.ds(at, rows), pl.ds(column, width)], sems.at[k]
            )
        )
    for copy in copies:
        copy.start()
    for copy in copies:
        copy.wait()


def assemble(ring, pieces):
    rows, columns = pieces[0][2].shape
    spans = tuple((column, piece.shape[1]) for _, column, piece in pieces)
    places = jnp.stack([ring.index(offset) * rows for offset, _, _ in pieces])
    size = ring.count * rows * columns * 2
    return pl.pallas_call(
        functools.partial(assemble_kernel, spans),
        in_specs=[SMEM] + [ANY] * len(spans),
        out_specs=ANY,
        out_shape=jax.ShapeDtypeStruct((ring.count * rows, columns), BF),
        scratch_shapes=[pltpu.SemaphoreType.DMA((len(spans),))],
        compiler_params=params(16),
        cost_estimate=cost(0, 2 * size),
        name="assemble",
    )(places.astype(jnp.int32), *[piece for _, _, piece in pieces])


def rope_rows(values, cosine, sine):
    first, second = values[:HALF], values[HALF:]
    return first * cosine - second * sine, second * cosine + first * sine


def project_kernel(query_heads, key_heads, x_ref, w_ref, c_ref, s_ref, o_ref):
    turned_heads = dot(x_ref[...], w_ref[...]).T
    cosine, sine = c_ref[...], s_ref[...]
    for h in range(query_heads + key_heads):
        first, second = rope_rows(turned_heads[h * HD : (h + 1) * HD], cosine, sine)
        if h < query_heads:
            first, second = first * (SCALE * LOG2E), second * (SCALE * LOG2E)
        o_ref[h * HD : h * HD + HALF, :] = first.astype(BF)
        o_ref[h * HD + HALF : (h + 1) * HD, :] = second.astype(BF)
    done = (query_heads + key_heads) * HD
    o_ref[done:, :] = turned_heads[done:].astype(BF)


def project(x, w, cosine, sine, query_heads, key_heads, block):
    n, d = x.shape
    columns = (query_heads + 2 * key_heads) * HD
    return pl.pallas_call(
        functools.partial(project_kernel, query_heads, key_heads),
        grid=(n // block,),
        in_specs=[
            pl.BlockSpec((block, d), lambda i: (i, 0)),
            pl.BlockSpec((d, columns), lambda i: (0, 0)),
            pl.BlockSpec((HALF, block), lambda i: (0, i)),
            pl.BlockSpec((HALF, block), lambda i: (0, i)),
        ],
        out_specs=pl.BlockSpec((columns, block), lambda i: (0, i)),
        out_shape=jax.ShapeDtypeStruct((columns, n), BF),
        compiler_params=params(40),
        cost_estimate=cost(2 * n * d * columns, 2 * (n * d + d * columns + n * columns)),
        name="project",
    )(x, w, cosine, sine)


def side(ref, low, high):
    return jnp.concatenate(
        [ref[h * HD : (h + 1) * HD, low:high] for h in range(ref.shape[0] // HD)], axis=1
    )


def attend_kernel(block, q_ref, k_ref, v_ref, start_ref, o_ref, l_ref):
    n, group = q_ref.shape[1], q_ref.shape[0] // HD
    keys = turned(k_ref[...]).astype(BF)
    row = lax.broadcasted_iota(jnp.int32, (block, group * block), 0)
    column = lax.broadcasted_iota(jnp.int32, (block, group * block), 1) % block
    for i in range(n // block):
        low, high = i * block, (i + 1) * block
        start = jnp.concatenate([start_ref[:, low:high]] * group, axis=1)
        scores = dot(keys[:high], side(q_ref, low, high))
        at = lax.broadcasted_iota(jnp.int32, (high, group * block), 0)
        scores = jnp.where(at >= start, scores, NEG)
        near = jnp.where(row <= column, scores[low:], NEG)
        top = jnp.max(near, axis=0, keepdims=True)
        if i:
            top = jnp.maximum(top, jnp.max(scores[:low], axis=0, keepdims=True))
        near = jnp.exp2(near - top)
        total = jnp.sum(near, axis=0, keepdims=True)
        out = dot(v_ref[:, low:high], near.astype(BF))
        if i:
            far = jnp.exp2(scores[:low] - top)
            total = total + jnp.sum(far, axis=0, keepdims=True)
            out = out + dot(v_ref[:, :low], far.astype(BF))
        out = out * (1.0 / total)
        log_total = top + jnp.log2(total)
        for h in range(group):
            part = slice(h * block, (h + 1) * block)
            o_ref[h * HD : (h + 1) * HD, low:high] = out[:, part].astype(BF)
            l_ref[0, h : h + 1, low:high] = log_total[:, part]


def attend(qkv, start, query_heads, key_heads, block):
    n, group = qkv.shape[1], query_heads // key_heads
    return pl.pallas_call(
        functools.partial(attend_kernel, block),
        grid=(key_heads,),
        in_specs=[
            pl.BlockSpec((group * HD, n), lambda i: (i, 0)),
            pl.BlockSpec((HD, n), lambda i: (query_heads + i, 0)),
            pl.BlockSpec((HD, n), lambda i: (query_heads + key_heads + i, 0)),
            pl.BlockSpec((1, n), lambda i: (0, 0)),
        ],
        out_specs=[
            pl.BlockSpec((group * HD, n), lambda i: (i, 0)),
            pl.BlockSpec((1, group, n), lambda i: (i, 0, 0)),
        ],
        out_shape=[
            jax.ShapeDtypeStruct((query_heads * HD, n), BF),
            jax.ShapeDtypeStruct((key_heads, group, n), F32),
        ],
        compiler_params=params(40),
        cost_estimate=cost(
            4 * n * n * HD * query_heads, 4 * n * HD * (query_heads + key_heads),
            n * n * query_heads // 2,
        ),
        name="attend",
    )(qkv, qkv, qkv, start)


def attend_back_kernel(
    block, q_ref, k_ref, v_ref, g_ref, h_ref, l_ref, start_ref, c_ref, s_ref,
    dq_ref, dk_ref, dv_ref, dk_sum, dv_sum,
):
    n, group = q_ref.shape[1], q_ref.shape[0] // HD
    keys = turned(k_ref[...]).astype(BF)
    values = turned(v_ref[...]).astype(BF)
    dk_sum[...] = jnp.zeros_like(dk_sum)
    dv_sum[...] = jnp.zeros_like(dv_sum)
    for i in range(n // block):
        low, high = i * block, (i + 1) * block
        queries, grads = side(q_ref, low, high), side(g_ref, low, high)
        outs = side(h_ref, low, high)
        query_rows, grad_rows = turned(queries).astype(BF), turned(grads).astype(BF)
        inner = jnp.sum(grads.astype(F32) * outs.astype(F32), axis=0, keepdims=True)
        log_total = jnp.concatenate([l_ref[0, h : h + 1, low:high] for h in range(group)], axis=1)
        start = jnp.concatenate([start_ref[:, low:high]] * group, axis=1)
        dq = jnp.zeros((HD, group * block), F32)
        for first, last in ([(0, low)] if i else []) + [(low, high)]:
            scores = dot(keys[first:last], queries)
            at = lax.broadcasted_iota(jnp.int32, scores.shape, 0) + first
            allowed = at >= start
            if first == low:
                column = lax.broadcasted_iota(jnp.int32, scores.shape, 1) % block + low
                allowed = allowed & (at <= column)
            probs = jnp.exp2(jnp.where(allowed, scores - log_total, NEG))
            dp = dot(values[first:last], grads)
            ds = (probs * (dp - inner)).astype(BF)
            dv_sum[first:last, :] += dot(probs.astype(BF), grad_rows)
            dk_sum[first:last, :] += dot(ds, query_rows)
            dq = dq + dot(k_ref[:, first:last], ds)
        dq = dq * SCALE
        cosine, sine = c_ref[:, low:high], s_ref[:, low:high]
        for h in range(group):
            top, bottom = rope_rows(dq[:, h * block : (h + 1) * block], cosine, -sine)
            dq_ref[h * HD : h * HD + HALF, low:high] = top.astype(BF)
            dq_ref[h * HD + HALF : (h + 1) * HD, low:high] = bottom.astype(BF)
    top, bottom = rope_rows(dk_sum[...].T * (1.0 / LOG2E), c_ref[...], -s_ref[...])
    dk_ref[:HALF, :] = top.astype(BF)
    dk_ref[HALF:, :] = bottom.astype(BF)
    dv_ref[...] = dv_sum[...].T.astype(BF)


def attend_back(qkv, grads, heads_out, log_total, start, cosine, sine, query_heads, key_heads, block):
    n, group = qkv.shape[1], query_heads // key_heads
    whole = lambda i: (0, 0)
    wide = pl.BlockSpec((group * HD, n), lambda i: (i, 0))
    narrow = pl.BlockSpec((HD, n), lambda i: (i, 0))
    return pl.pallas_call(
        functools.partial(attend_back_kernel, block),
        grid=(key_heads,),
        in_specs=[
            wide,
            pl.BlockSpec((HD, n), lambda i: (query_heads + i, 0)),
            pl.BlockSpec((HD, n), lambda i: (query_heads + key_heads + i, 0)),
            wide,
            wide,
            pl.BlockSpec((1, group, n), lambda i: (i, 0, 0)),
            pl.BlockSpec((1, n), whole),
            pl.BlockSpec((HALF, n), whole),
            pl.BlockSpec((HALF, n), whole),
        ],
        out_specs=[wide, narrow, narrow],
        out_shape=[
            jax.ShapeDtypeStruct((query_heads * HD, n), BF),
            jax.ShapeDtypeStruct((key_heads * HD, n), BF),
            jax.ShapeDtypeStruct((key_heads * HD, n), BF),
        ],
        scratch_shapes=[pltpu.VMEM((n, HD), F32), pltpu.VMEM((n, HD), F32)],
        compiler_params=params(40),
        cost_estimate=cost(
            10 * n * n * HD * query_heads, 8 * n * HD * (query_heads + key_heads),
            n * n * query_heads // 2,
        ),
        name="attend_back",
    )(qkv, qkv, qkv, grads, heads_out, log_total, start, cosine, sine)


def columns_of(ref, place, block):
    return ref[:, pl.ds(pl.multiple_of(place * block, block), block)]


def branch_kernel(place_ref, h_ref, w_ref, *out_refs):
    for k, out in enumerate(out_refs):
        heads = turned(columns_of(h_ref, place_ref[k], out.shape[0])).astype(BF)
        out[...] = dot_nt(heads, w_ref[...]).astype(BF)


def branch(places, heads_out, w_full, width, rows):
    depth = heads_out.shape[0]
    first = w_full.shape[1] // depth - 1
    d = w_full.shape[0]
    return pl.pallas_call(
        branch_kernel,
        grid=(1,),
        in_specs=[
            SMEM,
            pl.BlockSpec(heads_out.shape, lambda i: (0, 0)),
            pl.BlockSpec((d, depth), lambda i: (0, first)),
        ],
        out_specs=[pl.BlockSpec((rows, d), lambda i: (0, 0))] * len(places),
        out_shape=[jax.ShapeDtypeStruct((rows, d), BF)] * len(places),
        compiler_params=params(40),
        cost_estimate=cost(2 * rows * len(places) * d * depth, 2 * d * (depth + 2 * rows)),
        name="branch",
    )(jnp.stack(places), heads_out, w_full)


def gate_up_kernel(x0_ref, x1_ref, w_ref, act_ref, a_ref, b_ref, x_all):
    rows, half = x0_ref.shape[0], w_ref.shape[1] // 2

    @pl.when(pl.program_id(0) == 0)
    def _():
        x_all[:rows] = x0_ref[...]
        x_all[rows:] = x1_ref[...]

    product = dot(x_all[...], w_ref[...])
    gate, up = product[:, :half], product[:, half:]
    sigmoid = 1.0 / (1.0 + jnp.exp(-gate))
    silu = gate * sigmoid
    act_ref[...] = (silu * up).astype(BF)
    a_ref[...] = (up * sigmoid * (1.0 + gate * (1.0 - sigmoid))).astype(BF)
    b_ref[...] = silu.astype(BF)


def gate_up(x0, x1, w, block):
    rows, d = x0.shape
    units = w.shape[1] // 2
    out = pl.BlockSpec((2 * rows, block), lambda j: (0, j))
    whole = pl.BlockSpec((rows, d), lambda j: (0, 0))
    return pl.pallas_call(
        gate_up_kernel,
        grid=(units // block,),
        in_specs=[whole, whole, pl.BlockSpec((d, 2 * block), lambda j: (0, j))],
        out_specs=[out] * 3,
        out_shape=[jax.ShapeDtypeStruct((2 * rows, units), BF)] * 3,
        scratch_shapes=[pltpu.VMEM((2 * rows, d), BF)],
        compiler_params=params(40),
        cost_estimate=cost(8 * rows * d * units, 4 * (d * units + rows * d), 2 * rows * units),
        name="gate_up",
    )(x0, x1, w)


def mlp_back_kernel(g0_ref, g1_ref, a_ref, b_ref, wd_ref, w_ref, d_ref, u0_ref, u1_ref, g_all, total):
    rows, half = g0_ref.shape[0], a_ref.shape[1]
    step = pl.program_id(0)

    @pl.when(step == 0)
    def _():
        g_all[:rows] = g0_ref[...]
        g_all[rows:] = g1_ref[...]

    grad_act = dot(g_all[...], wd_ref[...])
    d_ref[:, :half] = (grad_act * a_ref[...].astype(F32)).astype(BF)
    d_ref[:, half:] = (grad_act * b_ref[...].astype(F32)).astype(BF)
    part = dot_nt(d_ref[...], w_ref[...])

    @pl.when(step == 0)
    def _():
        total[...] = part

    @pl.when(step > 0)
    def _():
        total[...] += part

    @pl.when(step == pl.num_programs(0) - 1)
    def _():
        u0_ref[...] = total[:rows].astype(BF)
        u1_ref[...] = total[rows:].astype(BF)


def mlp_back(g0, g1, a, b, w_down, w, block):
    rows, d = g0.shape
    units = a.shape[1]
    whole = pl.BlockSpec((rows, d), lambda j: (0, 0))
    narrow = pl.BlockSpec((2 * rows, block), lambda j: (0, j))
    return pl.pallas_call(
        mlp_back_kernel,
        grid=(units // block,),
        in_specs=[
            whole, whole, narrow, narrow,
            pl.BlockSpec((d, block), lambda j: (0, j)),
            pl.BlockSpec((d, 2 * block), lambda j: (0, j)),
        ],
        out_specs=[pl.BlockSpec((2 * rows, 2 * block), lambda j: (0, j)), whole, whole],
        out_shape=[
            jax.ShapeDtypeStruct((2 * rows, 2 * units), BF),
            jax.ShapeDtypeStruct((rows, d), BF),
            jax.ShapeDtypeStruct((rows, d), BF),
        ],
        scratch_shapes=[pltpu.VMEM((2 * rows, d), BF), pltpu.VMEM((2 * rows, d), F32)],
        compiler_params=params(48),
        cost_estimate=cost(12 * rows * d * units, 6 * d * units + 12 * rows * (units + d)),
        name="mlp_back",
    )(g0, g1, a, b, w_down, w)


def weight_grad_kernel(x0_ref, x1_ref, x2_ref, x3_ref, d0_ref, d1_ref, o_ref, x_turned):
    rows = x0_ref.shape[0]

    @pl.when(pl.program_id(0) == 0)
    def _():
        for k, ref in enumerate((x0_ref, x1_ref, x2_ref, x3_ref)):
            x_turned[:, k * rows : (k + 1) * rows] = turned(ref[...]).astype(BF)

    both = 2 * rows
    o_ref[...] = (
        dot(x_turned[:, :both], d0_ref[...]) + dot(x_turned[:, both:], d1_ref[...])
    ).astype(BF)


def weight_grad(pieces, d0, d1, block):
    rows, d = pieces[0].shape
    columns = d0.shape[1]
    whole = pl.BlockSpec((rows, d), lambda j: (0, 0))
    narrow = pl.BlockSpec((2 * rows, block), lambda j: (0, j))
    return pl.pallas_call(
        weight_grad_kernel,
        grid=(columns // block,),
        in_specs=[whole] * 4 + [narrow] * 2,
        out_specs=pl.BlockSpec((d, block), lambda j: (0, j)),
        out_shape=jax.ShapeDtypeStruct((d, columns), BF),
        scratch_shapes=[pltpu.VMEM((d, 4 * rows), BF)],
        compiler_params=params(40),
        cost_estimate=cost(8 * rows * d * columns, 8 * rows * (d + columns) + 2 * d * columns),
        name="weight_grad",
    )(*pieces, d0, d1)


def down_kernel(act_ref, w_ref, o0_ref, o1_ref):
    rows = o0_ref.shape[0]
    out = dot_nt(act_ref[...], w_ref[...])
    o0_ref[...] = out[:rows].astype(BF)
    o1_ref[...] = out[rows:].astype(BF)


def down(act, w_down, block):
    both, units = act.shape
    d = w_down.shape[0]
    out = pl.BlockSpec((both // 2, block), lambda j: (0, j))
    return pl.pallas_call(
        down_kernel,
        grid=(d // block,),
        in_specs=[
            pl.BlockSpec((both, units), lambda j: (0, 0)),
            pl.BlockSpec((block, units), lambda j: (j, 0)),
        ],
        out_specs=[out, out],
        out_shape=[jax.ShapeDtypeStruct((both // 2, d), BF)] * 2,
        compiler_params=params(40),
        cost_estimate=cost(2 * both * d * units, 2 * (both * units + d * units + both * d)),
        name="down",
    )(act, w_down)


def grad_heads_kernel(place_ref, g0_ref, g1_ref, g2_ref, g3_ref, w_ref, o_ref):
    for k, ref in enumerate((g0_ref, g1_ref, g2_ref, g3_ref)):
        rows = ref.shape[0]
        at = pl.multiple_of(place_ref[k] * rows, rows)
        o_ref[:, pl.ds(at, rows)] = dot(ref[...], w_ref[...]).T.astype(BF)


def grad_heads(places, pieces, w_full, depth):
    rows, d = pieces[0].shape
    first = w_full.shape[1] // depth - 1
    whole = pl.BlockSpec((rows, d), lambda i: (0, 0))
    return pl.pallas_call(
        grad_heads_kernel,
        grid=(1,),
        in_specs=[SMEM] + [whole] * 4 + [pl.BlockSpec((d, depth), lambda i: (0, first))],
        out_specs=pl.BlockSpec((depth, 4 * rows), lambda i: (0, 0)),
        out_shape=jax.ShapeDtypeStruct((depth, 4 * rows), BF),
        compiler_params=params(40),
        cost_estimate=cost(8 * rows * d * depth, 2 * d * (depth + 4 * rows)),
        name="grad_heads",
    )(jnp.stack(places), *pieces, w_full)


def grad_x_kernel(place_ref, q_ref, k_ref, v_ref, w_ref, *out_refs):
    for k, out in enumerate(out_refs):
        rows = out.shape[0]
        parts = [columns_of(ref, place_ref[k], rows).astype(F32) for ref in (q_ref, k_ref, v_ref)]
        grads = jnp.concatenate(parts, axis=0).T.astype(BF)
        out[...] = dot_nt(grads, w_ref[...]).astype(BF)


def grad_x(places, dq, dk, dv, w_full, rows):
    d = w_full.shape[0]
    columns = dq.shape[0] + dk.shape[0] + dv.shape[0]
    whole = lambda i: (0, 0)
    return pl.pallas_call(
        grad_x_kernel,
        grid=(1,),
        in_specs=[
            SMEM,
            pl.BlockSpec(dq.shape, whole),
            pl.BlockSpec(dk.shape, whole),
            pl.BlockSpec(dv.shape, whole),
            pl.BlockSpec((d, columns), whole),
        ],
        out_specs=[pl.BlockSpec((rows, d), whole)] * len(places),
        out_shape=[jax.ShapeDtypeStruct((rows, d), BF)] * len(places),
        compiler_params=params(40),
        cost_estimate=cost(2 * rows * len(places) * d * columns, 2 * columns * (d + 4 * rows)),
        name="grad_x",
    )(jnp.stack(places), dq, dk, dv, w_full)


def attn_grad_kernel(
    place_ref, x_ref, q_ref, k_ref, v_ref, h_ref, g0_ref, g1_ref, g2_ref, g3_ref, o_ref
):
    at = 0
    for ref in (q_ref, k_ref, v_ref):
        size = ref.shape[0]
        o_ref[:, at : at + size] = dot(ref[...], x_ref[...]).T.astype(BF)
        at += size
    total = None
    for k, ref in enumerate((g0_ref, g1_ref, g2_ref, g3_ref)):
        part = dot(columns_of(h_ref, place_ref[k], ref.shape[0]), ref[...])
        total = part if total is None else total + part
    o_ref[:, at:] = total.T.astype(BF)


def attn_grad(places, x, dq, dk, dv, heads_out, pieces):
    n, d = x.shape
    rows = pieces[0].shape[0]
    columns = dq.shape[0] + dk.shape[0] + dv.shape[0] + heads_out.shape[0]
    whole = lambda i: (0, 0)
    arrays = (x, dq, dk, dv, heads_out, *pieces)
    return pl.pallas_call(
        attn_grad_kernel,
        grid=(1,),
        in_specs=[SMEM] + [pl.BlockSpec(a.shape, whole) for a in arrays],
        out_specs=pl.BlockSpec((d, columns), whole),
        out_shape=jax.ShapeDtypeStruct((d, columns), BF),
        compiler_params=params(48),
        cost_estimate=cost(2 * n * d * columns, 2 * (2 * n * d + n * columns + d * columns)),
        name="attn_grad",
    )(jnp.stack(places), *arrays)


class Ring:
    def __init__(self, count):
        self.count = count
        self.half = count // 2
        order = [2 * k if k < self.half else 2 * (count - 1 - k) + 1 for k in range(count)]
        self.right = [(order[k], order[(k + 1) % count]) for k in range(count)]
        self.left = [(b, a) for a, b in self.right]
        me = lax.axis_index("dp")
        self.place = jnp.where(me % 2 == 0, me // 2, count - 1 - me // 2)

    def index(self, offset):
        place = (self.place + offset + self.count) % self.count
        return jnp.where(place < self.half, 2 * place, 2 * (self.count - 1 - place) + 1)

    def go_right(self, value):
        return lax.ppermute(value, "dp", self.right)

    def go_left(self, value):
        return lax.ppermute(value, "dp", self.left)


def cut_of(columns):
    return max(128, (columns // 2 + 127) // 128 * 128)


def gather_pieces(ring, shard):
    cut = cut_of(shard.shape[1])
    pieces = [(0, 0, shard)]
    from_left = from_right = shard
    for step in range(1, ring.half):
        from_left = ring.go_right(from_left)
        from_right = ring.go_left(from_right)
        pieces += [(-step, 0, from_left), (step, 0, from_right)]
    pieces.append((-ring.half, 0, ring.go_right(from_left[:, :cut])))
    pieces.append((ring.half, cut, ring.go_left(from_right[:, cut:])))
    return pieces


def scatter_sum(ring, whole):
    rows, columns = whole.shape[0] // ring.count, whole.shape[1]
    cut = cut_of(columns)

    def chunk(offset):
        return lax.dynamic_slice(whole, (ring.index(offset) * rows, 0), (rows, columns))

    far = chunk(ring.half)
    from_left = ring.go_right(far[:, :cut])
    from_right = ring.go_left(far[:, cut:])
    for step in range(ring.half - 1, 0, -1):
        to_right, to_left = chunk(step).astype(F32), chunk(-step).astype(F32)
        if step == ring.half - 1:
            to_right = jnp.concatenate(
                [to_right[:, :cut] + from_left.astype(F32), to_right[:, cut:]], axis=1
            )
            to_left = jnp.concatenate(
                [to_left[:, :cut], to_left[:, cut:] + from_right.astype(F32)], axis=1
            )
        else:
            to_right = to_right + from_left.astype(F32)
            to_left = to_left + from_right.astype(F32)
        from_left = ring.go_right(to_right.astype(BF))
        from_right = ring.go_left(to_left.astype(BF))
    return chunk(0).astype(F32) + from_left.astype(F32) + from_right.astype(F32)


def swap_core(value):
    return lax.ppermute(value, "tensor", CORE_PAIRS)


def swap_x(value):
    return lax.ppermute(value, "tensor", X_PAIRS)


def gather_tokens(own):
    across = swap_x(own)
    return own, swap_core(own), across, swap_core(across)


def plus(left_side, right_side):
    return (left_side.astype(F32) + right_side.astype(F32)).astype(BF)


def sum_both(own, mate, across, far):
    across_chip = plus(across, swap_core(far))
    own_theirs = swap_x(across_chip)
    own_chip = plus(own, swap_core(mate))
    across_theirs = swap_x(own_chip)
    return (
        own_chip.astype(F32) + own_theirs.astype(F32),
        across_chip.astype(F32) + across_theirs.astype(F32),
    )


def sum_own(own, mate, across, far):
    theirs = swap_x(plus(across, swap_core(far)))
    return own.astype(F32) + swap_core(mate).astype(F32) + theirs.astype(F32)


def rope_tables(segment):
    places = jnp.arange(segment.shape[0], dtype=jnp.int32)
    previous = jnp.concatenate([segment[:1] - 1, segment[:-1]])
    opening = lax.cummax(jnp.where(segment != previous, places, 0), axis=0)
    position = (places - opening).astype(F32)
    inverse = jnp.exp(-(2.0 * jnp.arange(HALF, dtype=F32) / HD) * math.log(THETA))
    angle = inverse[:, None] * position[None, :]
    return jnp.cos(angle), jnp.sin(angle), opening[None, :]


def inverse_rms(values):
    return lax.rsqrt(jnp.mean(values * values, axis=-1, keepdims=True) + EPS)


def norm_back(scaled, values, inverse):
    return inverse * scaled - values * inverse * inverse * inverse * jnp.mean(
        scaled * values, axis=-1, keepdims=True
    )


def interleave(left_side, right_side, block):
    rows, columns = left_side.shape
    both = jnp.stack(
        [left_side.reshape(rows, -1, block), right_side.reshape(rows, -1, block)], axis=2
    )
    return both.reshape(rows, 2 * columns)


def separate(both, block):
    rows, columns = both.shape
    both = both.reshape(rows, -1, 2, block)
    return both[:, :, 0].reshape(rows, columns // 2), both[:, :, 1].reshape(rows, columns // 2)


def per_device(
    dp_count,
    hidden_in,
    segments,
    attn_gain,
    w_query,
    w_key,
    w_value,
    w_out,
    mlp_gain,
    w_gate,
    w_up,
    w_down,
    cotangent,
):
    ring = Ring(dp_count)
    device = lax.axis_index("tensor").astype(jnp.int32)
    places = [device ^ k for k in range(4)]
    rows, width = hidden_in.shape
    query_columns, key_columns = w_query.shape[1], w_key.shape[1]
    query_heads, key_heads = query_columns // HD, key_columns // HD
    qkv_columns = query_columns + 2 * key_columns
    block = min(256, w_gate.shape[1])
    gain_one = attn_gain.astype(F32)[:, None]
    gain_two = mlp_gain.astype(F32)[:, None]

    w_qkv = jnp.concatenate([w_query, w_key, w_value], axis=1)
    w_gate_up = interleave(w_gate, w_up, block)
    shard_qkv = (w_qkv.astype(F32) * gain_one).astype(BF)
    shard_gate_up = (w_gate_up.astype(F32) * gain_two).astype(BF)
    pieces_attn = gather_pieces(ring, jnp.concatenate([shard_qkv, w_out.T], axis=1))
    full_attn = assemble(ring, pieces_attn)
    full_gate_up = assemble(ring, gather_pieces(ring, shard_gate_up))
    full_down = assemble(ring, gather_pieces(ring, w_down.T))

    hidden = gather_tokens(hidden_in)
    grads = gather_tokens(cotangent)
    normed = jnp.zeros((4 * rows, width), BF)
    for piece, at in zip(hidden, places):
        part = piece.astype(F32)
        part = (part * inverse_rms(part)).astype(BF)
        normed = lax.dynamic_update_slice(normed, part, (at * rows, 0))
    cosine, sine, start = rope_tables(segments)
    qkv = project(normed, full_attn, cosine, sine, query_heads, key_heads, rows)
    heads_out, log_total = attend(qkv, start, query_heads, key_heads, rows)

    across_part, far_part = branch([places[2], places[3]], heads_out, full_attn, width, rows)
    own_part, mate_part = branch([places[0], places[1]], heads_out, full_attn, width, rows)
    sums = sum_both(own_part, mate_part, across_part, far_part)
    resid = [hidden[2 * k].astype(F32) + sums[k] for k in range(2)]
    inverse_two = [inverse_rms(value) for value in resid]
    normed_two, mlp = [], []
    for k in range(2):
        part = (resid[k] * inverse_two[k]).astype(BF)
        normed_two += [part, swap_core(part)]
        mlp.append(gate_up(part, normed_two[-1], full_gate_up, block))
    down_parts = [down(mlp[k][0], full_down, 256) for k in range(2)]
    output = resid[0] + sum_own(*down_parts[0], *down_parts[1])

    grad_down_w = scatter_sum(ring, weight_grad(grads, mlp[0][0], mlp[1][0], 2 * block))
    back = [
        mlp_back(grads[2 * k], grads[2 * k + 1], mlp[k][1], mlp[k][2], full_down, full_gate_up, block)
        for k in range(2)
    ]
    grad_gate_up_w = scatter_sum(ring, weight_grad(normed_two, back[0][0], back[1][0], 2 * block))
    sums = sum_both(*back[0][1:], *back[1][1:])
    grad_resid, grad_branch = [], []
    for k in range(2):
        grad_resid.append(
            grads[2 * k].astype(F32) + norm_back(sums[k], resid[k], inverse_two[k])
        )
        part = grad_resid[k].astype(BF)
        grad_branch += [part, swap_core(part)]

    grad_out = grad_heads(places, grad_branch, full_attn, query_columns)
    dq, dk, dv = attend_back(
        qkv, grad_out, heads_out, log_total, start, cosine, sine, query_heads, key_heads, rows
    )
    across_part, far_part = grad_x([places[2], places[3]], dq, dk, dv, full_attn, rows)
    own_part, mate_part = grad_x([places[0], places[1]], dq, dk, dv, full_attn, rows)
    scaled_one = sum_own(own_part, mate_part, across_part, far_part)
    grad_attn_w = scatter_sum(
        ring, attn_grad(places, normed, dq, dk, dv, heads_out, grad_branch)
    )
    own = hidden_in.astype(F32)
    hidden_grad = (grad_resid[0] + norm_back(scaled_one, own, inverse_rms(own))).astype(BF)

    grad_qkv_w = grad_attn_w[:, :qkv_columns]
    gain_parts = jnp.stack(
        [
            jnp.sum(grad_qkv_w * w_qkv.astype(F32), axis=1),
            jnp.sum(grad_gate_up_w * w_gate_up.astype(F32), axis=1),
        ]
    )
    gain_sums = lax.psum(gain_parts, "tensor")
    grad_qkv_w = grad_qkv_w * gain_one
    grad_gate_w, grad_up_w = separate(grad_gate_up_w * gain_two, block)
    return (
        output.astype(BF),
        hidden_grad,
        gain_sums[0],
        grad_qkv_w[:, :query_columns],
        grad_qkv_w[:, query_columns : query_columns + key_columns],
        grad_qkv_w[:, query_columns + key_columns :],
        grad_attn_w[:, qkv_columns:].T,
        gain_sums[1],
        grad_gate_w,
        grad_up_w,
        grad_down_w.T,
    )


def solution(mesh):
    tokens, split = P(("dp", "tensor"), None), P("dp", "tensor")
    in_specs = (
        tokens, P("dp"), P("dp"), split, split, split, P("tensor", "dp"),
        P("dp"), split, split, P("tensor", "dp"), tokens,
    )
    out_specs = (
        tokens, tokens, P("dp"), split, split, split, P("tensor", "dp"),
        P("dp"), split, split, P("tensor", "dp"),
    )
    body = functools.partial(per_device, mesh.shape["dp"])
    return jax.shard_map(body, mesh=mesh, in_specs=in_specs, out_specs=out_specs, check_vma=False)
```

time: 520 us -> 450 us (0.87)
  matrix products: 106 us -> 0 us
  Pallas kernels: 0 us -> 103 us
  local copies, waits for them, and re-layouts: 93.5 us -> 51.5 us
  loops' own time: 12.6 us -> 0 us
  waiting for transfers between devices: 170 us -> 161 us
    dot_general x26 -> x0, matrix products: 106 us -> none  [the longest x4 28.2 us: matmul(): return jnp.dot(left_side, right_side, preferred_element_type=F32)]
    pallas_call x0 -> x20, Pallas kernels: none -> 103 us  [the longest x2 24.8 us: mlp_back(): pl.pallas_call(mlp_back_kernel, grid=(units // block,), in_specs=[whole,...]
    dynamic_update_slice x28 -> x0, local copies, waits for them, and re-layouts: 60 us -> none  [the longest x4 31.4 us: attend_back(): lax.scan(one_block, (empty_grad, empty_grad), (indices, log_totals))]
    unnamed x78 -> x236, local copies, waits for them, and re-layouts: 4.32 us -> 31.7 us
    ppermute x24, waiting for transfers between devices: 86.2 us -> 111 us  [go_right(): return lax.ppermute(value, 'dp', self.right)]
    ppermute x24, waiting for transfers between devices: 59.3 us -> 35.2 us  [go_left(): return lax.ppermute(value, 'dp', self.left)]
    another operation x2 -> x0, loops' own time: 12.6 us -> none  [the longest x1 10.8 us: attend(): lax.map(one_block, jnp.arange(length // block_rows, dtype=jnp.int32))]
    ppermute x8, waiting for transfers between devices: 22.1 us -> 14.2 us  [swap_x(): return lax.ppermute(value, 'tensor', X_PAIRS)]
  transfers between devices with their start and end apart: 72 -> 72, of which waited for: 33 -> 26; matrix products, arithmetic and copies ran while one was open for 37% -> 16% of each run, Pallas kernels for 0% -> 23%
where the time goes in v2:
time: 450 us; the launch traced here: 442 us
  waiting for transfers between devices  161 us (36%)
  Pallas kernels  103 us (23%)
  starting transfers between devices  62 us (14%)
  other arithmetic  55 us (12%)
  local copies, waits for them, and re-layouts  51.5 us (11%)
  blocking collectives  5.67 us (1%)
    ppermute x24, waiting for transfers between devices, go_right(): return lax.ppermute(value, 'dp', self.right)  111 us
    ppermute x24, waiting for transfers between devices, go_left(): return lax.ppermute(value, 'dp', self.left)  35.2 us
    unnamed x236, local copies, waits for them, and re-layouts  31.7 us
    ppermute x24, starting transfers between devices, go_right(): return lax.ppermute(value, 'dp', self.right)  30.7 us
    pallas_call x2, Pallas kernels, mlp_back(): pl.pallas_call(mlp_back_kernel, grid=(units // block,), in_specs=[whole,...  24.8 us
    ppermute x24, starting transfers between devices, go_left(): return lax.ppermute(value, 'dp', self.left)  21.6 us
    pallas_call x2, Pallas kernels, weight_grad(): pl.pallas_call(weight_grad_kernel, grid=(columns // block,), in_specs=[wh...  17.3 us
    ppermute x8, waiting for transfers between devices, swap_x(): return lax.ppermute(value, 'tensor', X_PAIRS)  14.2 us
  transfers between devices with their start and end apart: 72, of which 26 were waited for; matrix products, arithmetic and copies ran while one was open for 16% of the time, Pallas kernels for 23%

profile of v2, /device:TPU:0, one launch (start us, length us, event | category | flops | bytes accessed | tf_op | source)
XLA Modules:
  0.0 441.8 jit_solution(4257144196739153287)
XLA Ops:
  29.9 16.6 %collective-permute-done.5.refs_3_ = bf16[192,1152]{1,0:T(8,128)(2,1)S(1)} collective-permute-done((bf16[192,1152]{1,0:T(8,128)(2,1)S(1)}, bf16[192,1152]{1,0:T(8,128)(2,1)S(1)}, u32[]{:S(2)}, u32[]{:S(2)}) %collective-permute-start.5) | collective-permute-done | bytes 442400 | tf_op jit(solution)/shard_map/ppermute | solution.py:549
  67.2 5.1 %collective-permute-done.10.refs_8_ = bf16[192,512]{1,0:T(8,128)(2,1)S(1)} collective-permute-done((bf16[192,512]{1,0:T(8,128)(2,1)S(1)}, bf16[192,512]{1,0:T(8,128)(2,1)S(1)}, u32[]{:S(2)}, u32[]{:S(2)}) %collective-permute-start.10) | collective-permute-done | bytes 196640 | tf_op jit(solution)/shard_map/ppermute | solution.py:552
  82.0 4.9 %attend.1 = (bf16[384,1024]{1,0:T(8,128)(2,1)S(1)}, f32[2,2,1024]{2,1,0:T(2,128)S(1)}) custom-call(bf16[768,1024]{1,0:T(8,128)(2,1)S(1)} %project.1.q_ref.k_ref.v_ref, bf16[768,1024]{1,0:T(8,128)(2,1)S(1)} %project.1.q_ref.k_ref.v_ref, bf16[768,1024]{1,0:T(8,128)(2,1)S(1)} %project.1.q_ref.k_ref.v_ref, s32[1,1024]{1,0:T(1,128)S(1)} %bitcast.38), custom_call_target="tpu_custom_call" | custom-call | flops 1610612736 | bytes 2359296 | tf_op jit(solution)/shard_map/attend/pallas_call | solution.py:167
  90.7 9.4 %collective-permute-done.25.refs_3_ = bf16[192,1024]{1,0:T(8,128)(2,1)S(1)} collective-permute-done((bf16[192,1024]{1,0:T(8,128)(2,1)S(1)}, bf16[192,1024]{1,0:T(8,128)(2,1)S(1)}, u32[]{:S(2)}, u32[]{:S(2)}) %collective-permute-start.25) | collective-permute-done | bytes 393248 | tf_op jit(solution)/shard_map/ppermute | solution.py:549
  116.8 10.9 %collective-permute-done.19.refs_5_ = bf16[192,2048]{1,0:T(8,128)(2,1)S(1)} collective-permute-done((bf16[192,2048]{1,0:T(8,128)(2,1)S(1)}, bf16[192,2048]{1,0:T(8,128)(2,1)S(1)}, u32[]{:S(2)}, u32[]{:S(2)}) %collective-permute-start.19) | collective-permute-done | bytes 786464 | tf_op jit(solution)/shard_map/ppermute | solution.py:549
  137.5 8.4 %collective-permute-done.38.g0_ref.x2_ref = bf16[256,1536]{1,0:T(8,128)(2,1)S(1)} collective-permute-done((bf16[256,1536]{1,0:T(8,128)(2,1)S(1)}, bf16[256,1536]{1,0:T(8,128)(2,1)S(1)}, u32[]{:S(2)}, u32[]{:S(2)}) %collective-permute-start.38) | collective-permute-done | bytes 786464 | tf_op jit(solution)/shard_map/ppermute | solution.py:604
  169.1 5.5 %gate_up.2 = (bf16[512,1024]{1,0:T(8,128)(2,1)S(1)}, bf16[512,1024]{1,0:T(8,128)(2,1)S(1)}, bf16[512,1024]{1,0:T(8,128)(2,1)S(1)}) custom-call(bf16[256,1536]{1,0:T(8,128)(2,1)S(1)} %multiply_convert_fusion.2.x0_ref, bf16[256,1536]{1,0:T(8,128)(2,1)S(1)} %collective-permute-done.14.x1_ref, bf16[1536,2048]{1,0:T(8,128)(2,1)S(1)} %assemble.4.w_ref), custom_call_target="tpu_custom_call" | custom-call | flops 3221225472 | bytes 7864320 | tf_op jit(solution)/shard_map/gate_up/pallas_call | solution.py:323
  180.1 12.4 %mlp_back.2 = (bf16[512,2048]{1,0:T(8,128)(2,1)}, bf16[256,1536]{1,0:T(8,128)(2,1)S(1)}, bf16[256,1536]{1,0:T(8,128)(2,1)}) custom-call(bf16[256,1536]{1,0:T(8,128)(2,1)S(1)} %copy-done.44, bf16[256,1536]{1,0:T(8,128)(2,1)} %collective-permute-done.36.g1_ref.x1_ref, bf16[512,1024]{1,0:T(8,128)(2,1)S(1)} %copy-done.84, bf16[512,1024]{1,0:T(8,128)(2,1)S(1)} %copy-done.86, ...), custom_call_target="tpu_custom_call" | custom-call | flops 4831838208 | bytes 17301504 | tf_op jit(solution)/shard_map/mlp_back/pallas_call | solution.py:369
  201.8 6.6 %gate_up.3 = (bf16[512,1024]{1,0:T(8,128)(2,1)S(1)}, bf16[512,1024]{1,0:T(8,128)(2,1)S(1)}, bf16[512,1024]{1,0:T(8,128)(2,1)S(1)}) custom-call(bf16[256,1536]{1,0:T(8,128)(2,1)S(1)} %multiply_convert_fusion.1.x0_ref.x2_ref, bf16[256,1536]{1,0:T(8,128)(2,1)} %collective-permute-done.33.x1_ref.x3_ref, bf16[1536,2048]{1,0:T(8,128)(2,1)S(1)} %copy-done.1), custom_call_target="tpu_custom_call" | custom-call | flops 3221225472 | bytes 7864320 | tf_op jit(solution)/shard_map/gate_up/pallas_call | solution.py:323
  208.5 7.3 %weight_grad.3 = bf16[1536,1024]{1,0:T(8,128)(2,1)S(1)} custom-call(bf16[256,1536]{1,0:T(8,128)(2,1)S(1)} %copy-done.45, bf16[256,1536]{1,0:T(8,128)(2,1)} %collective-permute-done.36.g1_ref.x1_ref, bf16[256,1536]{1,0:T(8,128)(2,1)S(1)} %copy-done.25, bf16[256,1536]{1,0:T(8,128)(2,1)} %collective-permute-done.39.g1_ref.x3_ref, ...), custom_call_target="tpu_custom_call" | custom-call | flops 3221225472 | bytes 8388608 | tf_op jit(solution)/shard_map/weight_grad/pallas_call | solution.py:409
  222.9 12.4 %mlp_back.3 = (bf16[512,2048]{1,0:T(8,128)(2,1)}, bf16[256,1536]{1,0:T(8,128)(2,1)S(1)}, bf16[256,1536]{1,0:T(8,128)(2,1)}) custom-call(bf16[256,1536]{1,0:T(8,128)(2,1)S(1)} %copy-done.25, bf16[256,1536]{1,0:T(8,128)(2,1)} %collective-permute-done.39.g1_ref.x3_ref, bf16[512,1024]{1,0:T(8,128)(2,1)S(1)} %copy-done.80, bf16[512,1024]{1,0:T(8,128)(2,1)S(1)} %copy-done.82, ...), custom_call_target="tpu_custom_call" | custom-call | flops 4831838208 | bytes 17301504 | tf_op jit(solution)/shard_map/mlp_back/pallas_call | solution.py:369
  241.5 10.1 %weight_grad.2 = bf16[1536,2048]{1,0:T(8,128)(2,1)S(1)} custom-call(bf16[256,1536]{1,0:T(8,128)(2,1)S(1)} %copy-done.34, bf16[256,1536]{1,0:T(8,128)(2,1)S(1)} %copy-done.69, bf16[256,1536]{1,0:T(8,128)(2,1)S(1)} %multiply_convert_fusion.1.x0_ref.x2_ref, bf16[256,1536]{1,0:T(8,128)(2,1)} %collective-permute-done.33.x1_ref.x3_ref, ...), custom_call_target="tpu_custom_call" | custom-call | flops 6442450944 | bytes 13631488 | tf_op jit(solution)/shard_map/weight_grad/pallas_call | solution.py:409
  255.1 7.9 %collective-permute-done.56 = bf16[192,1024]{1,0:T(8,128)(2,1)S(1)} collective-permute-done((bf16[192,1024]{1,0:T(8,128)(2,1)S(1)}, bf16[192,1024]{1,0:T(8,128)(2,1)S(1)}, u32[]{:S(2)}, u32[]{:S(2)}) %collective-permute-start.56) | collective-permute-done | bytes 393248 | tf_op jit(solution)/shard_map/ppermute | solution.py:549
  266.4 8.2 %collective-permute-done.65 = bf16[192,1024]{1,0:T(8,128)(2,1)S(1)} collective-permute-done((bf16[192,1024]{1,0:T(8,128)(2,1)S(1)}, bf16[192,1024]{1,0:T(8,128)(2,1)S(1)}, u32[]{:S(2)}, u32[]{:S(2)}) %collective-permute-start.65) | collective-permute-done | bytes 393248 | tf_op jit(solution)/shard_map/ppermute | solution.py:549
  287.2 17.5 %collective-permute-done.66 = bf16[192,1024]{1,0:T(8,128)(2,1)S(1)} collective-permute-done((bf16[192,1024]{1,0:T(8,128)(2,1)S(1)}, bf16[192,1024]{1,0:T(8,128)(2,1)S(1)}, u32[]{:S(2)}, u32[]{:S(2)}) %collective-permute-start.66) | collective-permute-done | bytes 393248 | tf_op jit(solution)/shard_map/ppermute | solution.py:549
  307.5 6.9 %collective-permute-done.70 = bf16[192,1024]{1,0:T(8,128)(2,1)S(1)} collective-permute-done((bf16[192,1024]{1,0:T(8,128)(2,1)S(1)}, bf16[192,1024]{1,0:T(8,128)(2,1)S(1)}, u32[]{:S(2)}, u32[]{:S(2)}) %collective-permute-start.70) | collective-permute-done | bytes 393248 | tf_op jit(solution)/shard_map/ppermute | solution.py:552
  316.9 5.3 %collective-permute-done.35 = bf16[256,1536]{1,0:T(8,128)(2,1)S(1)} collective-permute-done((bf16[256,1536]{1,0:T(8,128)(2,1)S(1)}, bf16[256,1536]{1,0:T(8,128)(2,1)S(1)}, u32[]{:S(2)}, u32[]{:S(2)}) %collective-permute-start.35) | collective-permute-done | bytes 786464 | tf_op jit(solution)/shard_map/ppermute | solution.py:604
  331.6 11.5 %collective-permute-done.58 = bf16[192,2048]{1,0:T(8,128)(2,1)S(1)} collective-permute-done((bf16[192,2048]{1,0:T(8,128)(2,1)S(1)}, bf16[192,2048]{1,0:T(8,128)(2,1)S(1)}, u32[]{:S(2)}, u32[]{:S(2)}) %collective-permute-start.58) | collective-permute-done | bytes 786464 | tf_op jit(solution)/shard_map/ppermute | solution.py:549
  349.5 7.6 %attend_back.1 = (bf16[384,1024]{1,0:T(8,128)(2,1)S(1)}, bf16[192,1024]{1,0:T(8,128)(2,1)S(1)}, bf16[192,1024]{1,0:T(8,128)(2,1)S(1)}) custom-call(bf16[768,1024]{1,0:T(8,128)(2,1)S(1)} %copy-done.71, bf16[768,1024]{1,0:T(8,128)(2,1)S(1)} %copy-done.71, bf16[768,1024]{1,0:T(8,128)(2,1)S(1)} %copy-done.71, bf16[384,1024]{1,0:T(8,128)(2,1)S(1)} %grad_heads.1.g_ref, ...), custom_call_target="tpu_custom_call" | custom-call | flops 4026531840 | bytes 4718592 | tf_op jit(solution)/shard_map/attend_back/pallas_call | solution.py:241
  359.4 7.6 %attn_grad.1 = bf16[1536,1152]{1,0:T(8,128)(2,1)} custom-call(s32[4]{0:T(128)S(1)} %copy-done.67, bf16[1024,1536]{1,0:T(8,128)(2,1)} %copy-done.13, bf16[384,1024]{1,0:T(8,128)(2,1)S(1)} %get-tuple-element.60.q_ref, bf16[192,1024]{1,0:T(8,128)(2,1)S(1)} %get-tuple-element.61.k_ref, bf16[192,1024]{1,0:T(8,128)(2,1)S(1)} %get-tuple-element.62.v_ref, ...), custom_call_target="tpu_custom_call" | custom-call | flops 3623878656 | bytes 12189696 | tf_op jit(solution)/shard_map/attn_grad/pallas_call | solution.py:522
  381.7 10.0 %collective-permute-done.49 = bf16[192,1152]{1,0:T(8,128)(2,1)S(1)} collective-permute-done((bf16[192,1152]{1,0:T(8,128)(2,1)S(1)}, bf16[192,1152]{1,0:T(8,128)(2,1)S(1)}, u32[]{:S(2)}, u32[]{:S(2)}) %collective-permute-start.49) | collective-permute-done | bytes 442400 | tf_op jit(solution)/shard_map/ppermute | solution.py:549
  396.4 7.6 %collective-permute-done.50 = bf16[192,1152]{1,0:T(8,128)(2,1)S(1)} collective-permute-done((bf16[192,1152]{1,0:T(8,128)(2,1)S(1)}, bf16[192,1152]{1,0:T(8,128)(2,1)S(1)}, u32[]{:S(2)}, u32[]{:S(2)}) %collective-permute-start.50) | collective-permute-done | bytes 442400 | tf_op jit(solution)/shard_map/ppermute | solution.py:549
  407.3 4.9 %collective-permute-done.63 = bf16[192,2048]{1,0:T(8,128)(2,1)S(1)} collective-permute-done((bf16[192,2048]{1,0:T(8,128)(2,1)S(1)}, bf16[192,2048]{1,0:T(8,128)(2,1)S(1)}, u32[]{:S(2)}, u32[]{:S(2)}) %collective-permute-start.63) | collective-permute-done | bytes 786464 | tf_op jit(solution)/shard_map/ppermute | solution.py:552
  435.1 5.7 %psum.7 = f32[2,192]{1,0:T(2,128)S(1)} all-reduce(f32[2,192]{1,0:T(2,128)S(1)} %pad_maximum_fusion.8), channel_id=1, replica_groups=mesh['dp'=8,'tensor'=4] {'tensor'}, use_global_device_ids=true, to_apply=%region_13.14 | all-reduce | flops 384 | bytes 3072 | tf_op jit(solution)/shard_map/psum | solution.py:760
  (470 shorter events, 228.1 us)
Async XLA Ops:
  17.2 47.9 %collective-permute-start.15 = (bf16[192,2048]{1,0:T(8,128)(2,1)S(1)}, bf16[192,2048]{1,0:T(8,128)(2,1)}, u32[]{:S(2)}, u32[]{:S(2)}) collective-permute-start(bf16[192,2048]{1,0:T(8,128)(2,1)S(1)} %multiply_convert_fusion.refs_0_), channel_id=1, source_target_pairs={{0,8},{8,16},{16,24},{24,28},{28,20},{20,12},{12,4},{4,0},{1,9},{9... | collective-permute-start | bytes 2359304 | tf_op jit(solution)/shard_map/ppermute | solution.py:549
  22.6 43.0 %collective-permute-start.16 = (bf16[192,2048]{1,0:T(8,128)(2,1)S(1)}, bf16[192,2048]{1,0:T(8,128)(2,1)S(1)}, u32[]{:S(2)}, u32[]{:S(2)}) collective-permute-start(bf16[192,2048]{1,0:T(8,128)(2,1)S(1)} %multiply_convert_fusion.refs_0_), channel_id=1, source_target_pairs={{8,0},{16,8},{24,16},{28,24},{20,28},{12,20},{4,12},{0,4},{9,1},{1... | collective-permute-start | bytes 2359304 | tf_op jit(solution)/shard_map/ppermute | solution.py:552
  27.0 37.3 %collective-permute-start.2 = (bf16[256,1536]{1,0:T(8,128)(2,1)}, bf16[256,1536]{1,0:T(8,128)(2,1)S(1)}, u32[]{:S(2)}, u32[]{:S(2)}) collective-permute-start(bf16[256,1536]{1,0:T(8,128)(2,1)} %collective-permute-done.1), channel_id=1, source_target_pairs={{0,1},{1,0},{2,3},{3,2},{4,5},{5,4},{6,7},{7,6},{8,9},{9,8},{10,11... | collective-permute-start | bytes 2359304 | tf_op jit(solution)/shard_map/ppermute | solution.py:600
  57.9 30.7 %collective-permute-start.23 = (bf16[192,1024]{1,0:T(8,128)(2,1)S(1)}, bf16[192,1024]{1,0:T(8,128)(2,1)S(1)}, u32[]{:S(2)}, u32[]{:S(2)}) collective-permute-start(bf16[192,1024]{1,0:T(8,128)(2,1)S(1)} %bitcast.35), channel_id=1, source_target_pairs={{0,8},{8,16},{16,24},{24,28},{28,20},{20,12},{12,4},{4,0},{1,9},{9... | collective-permute-start | bytes 1179656 | tf_op jit(solution)/shard_map/ppermute | solution.py:549
  65.6 39.3 %collective-permute-start.17 = (bf16[192,2048]{1,0:T(8,128)(2,1)}, bf16[192,2048]{1,0:T(8,128)(2,1)S(1)}, u32[]{:S(2)}, u32[]{:S(2)}) collective-permute-start(bf16[192,2048]{1,0:T(8,128)(2,1)} %collective-permute-done.15.refs_1_), channel_id=1, source_target_pairs={{0,8},{8,16},{16,24},{24,28},{28,20},{20,12},{12,4},{4,0},{1,9},{9... | collective-permute-start | bytes 2359304 | tf_op jit(solution)/shard_map/ppermute | solution.py:549
  72.2 32.8 %collective-permute-start.18 = (bf16[192,2048]{1,0:T(8,128)(2,1)S(1)}, bf16[192,2048]{1,0:T(8,128)(2,1)S(1)}, u32[]{:S(2)}, u32[]{:S(2)}) collective-permute-start(bf16[192,2048]{1,0:T(8,128)(2,1)S(1)} %collective-permute-done.16.refs_2_), channel_id=1, source_target_pairs={{8,0},{16,8},{24,16},{28,24},{20,28},{12,20},{4,12},{0,4},{9,1},{1... | collective-permute-start | bytes 2359304 | tf_op jit(solution)/shard_map/ppermute | solution.py:552
  104.9 28.2 %collective-permute-start.11 = (bf16[256,1536]{1,0:T(8,128)(2,1)S(1)}, bf16[256,1536]{1,0:T(8,128)(2,1)S(1)}, u32[]{:S(2)}, u32[]{:S(2)}) collective-permute-start(bf16[256,1536]{1,0:T(8,128)(2,1)S(1)} %get-tuple-element.42), channel_id=1, source_target_pairs={{0,1},{1,0},{2,3},{3,2},{4,5},{5,4},{6,7},{7,6},{8,9},{9,8},{10,11... | collective-permute-start | bytes 2359304 | tf_op jit(solution)/shard_map/ppermute | solution.py:600
  114.9 31.0 %collective-permute-start.38 = (bf16[256,1536]{1,0:T(8,128)(2,1)S(1)}, bf16[256,1536]{1,0:T(8,128)(2,1)S(1)}, u32[]{:S(2)}, u32[]{:S(2)}) collective-permute-start(bf16[256,1536]{1,0:T(8,128)(2,1)S(1)} %copy-done.43), channel_id=1, source_target_pairs={{0,2},{2,0},{1,3},{3,1},{4,6},{6,4},{5,7},{7,5},{8,10},{10,8},{9,1... | collective-permute-start | bytes 2359304 | tf_op jit(solution)/shard_map/ppermute | solution.py:604
  148.0 29.7 %collective-permute-start.36 = (bf16[256,1536]{1,0:T(8,128)(2,1)}, bf16[256,1536]{1,0:T(8,128)(2,1)}, u32[]{:S(2)}, u32[]{:S(2)}) collective-permute-start(bf16[256,1536]{1,0:T(8,128)(2,1)} %x0_ref.1), channel_id=1, source_target_pairs={{0,1},{1,0},{2,3},{3,2},{4,5},{5,4},{6,7},{7,6},{8,9},{9,8},{10,11... | collective-permute-start | bytes 2359304 | tf_op jit(solution)/shard_map/ppermute | solution.py:600
  148.1 60.4 %collective-permute-start.39 = (bf16[256,1536]{1,0:T(8,128)(2,1)}, bf16[256,1536]{1,0:T(8,128)(2,1)}, u32[]{:S(2)}, u32[]{:S(2)}) collective-permute-start(bf16[256,1536]{1,0:T(8,128)(2,1)} %copy-done.24), channel_id=1, source_target_pairs={{0,1},{1,0},{2,3},{3,2},{4,5},{5,4},{6,7},{7,6},{8,9},{9,8},{10,11... | collective-permute-start | bytes 2359304 | tf_op jit(solution)/shard_map/ppermute | solution.py:600
  169.0 32.8 %collective-permute-start.33 = (bf16[256,1536]{1,0:T(8,128)(2,1)S(1)}, bf16[256,1536]{1,0:T(8,128)(2,1)}, u32[]{:S(2)}, u32[]{:S(2)}) collective-permute-start(bf16[256,1536]{1,0:T(8,128)(2,1)S(1)} %multiply_convert_fusion.1.x0_ref.x2_ref), channel_id=1, source_target_pairs={{0,1},{1,0},{2,3},{3,2},{4,5},{5,4},{6,7},{7,6},{8,9},{9,8},{10,11... | collective-permute-start | bytes 2359304 | tf_op jit(solution)/shard_map/ppermute | solution.py:600
  193.4 45.1 %collective-permute-start.37 = (bf16[256,1536]{1,0:T(8,128)(2,1)}, bf16[256,1536]{1,0:T(8,128)(2,1)}, u32[]{:S(2)}, u32[]{:S(2)}) collective-permute-start(bf16[256,1536]{1,0:T(8,128)(2,1)} %get-tuple-element.54), channel_id=1, source_target_pairs={{0,1},{1,0},{2,3},{3,2},{4,5},{5,4},{6,7},{7,6},{8,9},{9,8},{10,11... | collective-permute-start | bytes 2359304 | tf_op jit(solution)/shard_map/ppermute | solution.py:600
  201.8 115.0 %collective-permute-start.31 = (bf16[256,1536]{1,0:T(8,128)(2,1)}, bf16[256,1536]{1,0:T(8,128)(2,1)}, u32[]{:S(2)}, u32[]{:S(2)}) collective-permute-start(bf16[256,1536]{1,0:T(8,128)(2,1)} %get-tuple-element.47), channel_id=1, source_target_pairs={{0,1},{1,0},{2,3},{3,2},{4,5},{5,4},{6,7},{7,6},{8,9},{9,8},{10,11... | collective-permute-start | bytes 2359304 | tf_op jit(solution)/shard_map/ppermute | solution.py:600
  218.3 33.5 %collective-permute-start.64 = (bf16[192,512]{1,0:T(8,128)(2,1)}, bf16[192,512]{1,0:T(8,128)(2,1)}, u32[]{:S(2)}, u32[]{:S(2)}) collective-permute-start(bf16[192,512]{1,0:T(8,128)(2,1)} %get-tuple-element.99), channel_id=1, source_target_pairs={{0,8},{8,16},{16,24},{24,28},{28,20},{20,12},{12,4},{4,0},{1,9},{9... | collective-permute-start | bytes 589832 | tf_op jit(solution)/shard_map/ppermute | solution.py:549
  219.8 33.6 %collective-permute-start.68 = (bf16[192,512]{1,0:T(8,128)(2,1)}, bf16[192,512]{1,0:T(8,128)(2,1)}, u32[]{:S(2)}, u32[]{:S(2)}) collective-permute-start(bf16[192,512]{1,0:T(8,128)(2,1)} %get-tuple-element.101), channel_id=1, source_target_pairs={{8,0},{16,8},{24,16},{28,24},{20,28},{12,20},{4,12},{0,4},{9,1},{1... | collective-permute-start | bytes 589832 | tf_op jit(solution)/shard_map/ppermute | solution.py:552
  235.3 40.9 %collective-permute-start.40 = (bf16[256,1536]{1,0:T(8,128)(2,1)}, bf16[256,1536]{1,0:T(8,128)(2,1)}, u32[]{:S(2)}, u32[]{:S(2)}) collective-permute-start(bf16[256,1536]{1,0:T(8,128)(2,1)} %get-tuple-element.58), channel_id=1, source_target_pairs={{0,1},{1,0},{2,3},{3,2},{4,5},{5,4},{6,7},{7,6},{8,9},{9,8},{10,11... | collective-permute-start | bytes 2359304 | tf_op jit(solution)/shard_map/ppermute | solution.py:600
  240.0 37.9 %collective-permute-start.43 = (bf16[256,1536]{1,0:T(8,128)(2,1)S(1)}, bf16[256,1536]{1,0:T(8,128)(2,1)S(1)}, u32[]{:S(2)}, u32[]{:S(2)}) collective-permute-start(bf16[256,1536]{1,0:T(8,128)(2,1)S(1)} %add_convert_fusion.7), channel_id=1, source_target_pairs={{0,2},{2,0},{1,3},{3,1},{4,6},{6,4},{5,7},{7,5},{8,10},{10,8},{9,1... | collective-permute-start | bytes 2359304 | tf_op jit(solution)/shard_map/ppermute | solution.py:604
  276.2 55.4 %collective-permute-start.61 = (bf16[192,2048]{1,0:T(8,128)(2,1)S(1)}, bf16[192,2048]{1,0:T(8,128)(2,1)S(1)}, u32[]{:S(2)}, u32[]{:S(2)}) collective-permute-start(bf16[192,2048]{1,0:T(8,128)(2,1)S(1)} %pad_maximum_fusion.1), channel_id=1, source_target_pairs={{8,0},{16,8},{24,16},{28,24},{20,28},{12,20},{4,12},{0,4},{9,1},{1... | collective-permute-start | bytes 2359304 | tf_op jit(solution)/shard_map/ppermute | solution.py:552
  286.6 28.0 %collective-permute-start.41 = (bf16[256,1536]{1,0:T(8,128)(2,1)S(1)}, bf16[256,1536]{1,0:T(8,128)(2,1)S(1)}, u32[]{:S(2)}, u32[]{:S(2)}) collective-permute-start(bf16[256,1536]{1,0:T(8,128)(2,1)S(1)} %get-tuple-element.72), channel_id=1, source_target_pairs={{0,2},{2,0},{1,3},{3,1},{4,6},{6,4},{5,7},{7,5},{8,10},{10,8},{9,1... | collective-permute-start | bytes 2359304 | tf_op jit(solution)/shard_map/ppermute | solution.py:604
  314.5 32.5 %collective-permute-start.44 = (bf16[256,1536]{1,0:T(8,128)(2,1)S(1)}, bf16[256,1536]{1,0:T(8,128)(2,1)S(1)}, u32[]{:S(2)}, u32[]{:S(2)}) collective-permute-start(bf16[256,1536]{1,0:T(8,128)(2,1)S(1)} %add_convert_fusion.5.g2_ref), channel_id=1, source_target_pairs={{0,1},{1,0},{2,3},{3,2},{4,5},{5,4},{6,7},{7,6},{8,9},{9,8},{10,11... | collective-permute-start | bytes 2359304 | tf_op jit(solution)/shard_map/ppermute | solution.py:600
  344.9 34.9 %collective-permute-start.62 = (bf16[192,2048]{1,0:T(8,128)(2,1)}, bf16[192,2048]{1,0:T(8,128)(2,1)}, u32[]{:S(2)}, u32[]{:S(2)}) collective-permute-start(bf16[192,2048]{1,0:T(8,128)(2,1)} %get-tuple-element.82), channel_id=1, source_target_pairs={{8,0},{16,8},{24,16},{28,24},{20,28},{12,20},{4,12},{0,4},{9,1},{1... | collective-permute-start | bytes 2359304 | tf_op jit(solution)/shard_map/ppermute | solution.py:552
  346.5 59.1 %collective-permute-start.59 = (bf16[192,2048]{1,0:T(8,128)(2,1)}, bf16[192,2048]{1,0:T(8,128)(2,1)}, u32[]{:S(2)}, u32[]{:S(2)}) collective-permute-start(bf16[192,2048]{1,0:T(8,128)(2,1)} %get-tuple-element.81), channel_id=1, source_target_pairs={{0,8},{8,16},{16,24},{24,28},{28,20},{20,12},{12,4},{4,0},{1,9},{9... | collective-permute-start | bytes 2359304 | tf_op jit(solution)/shard_map/ppermute | solution.py:549
  375.3 49.2 %collective-permute-start.45 = (bf16[256,1536]{1,0:T(8,128)(2,1)}, bf16[256,1536]{1,0:T(8,128)(2,1)}, u32[]{:S(2)}, u32[]{:S(2)}) collective-permute-start(bf16[256,1536]{1,0:T(8,128)(2,1)} %get-tuple-element.64), channel_id=1, source_target_pairs={{0,1},{1,0},{2,3},{3,2},{4,5},{5,4},{6,7},{7,6},{8,9},{9,8},{10,11... | collective-permute-start | bytes 2359304 | tf_op jit(solution)/shard_map/ppermute | solution.py:600
  395.0 29.6 %collective-permute-start.47 = (bf16[256,1536]{1,0:T(8,128)(2,1)}, bf16[256,1536]{1,0:T(8,128)(2,1)}, u32[]{:S(2)}, u32[]{:S(2)}) collective-permute-start(bf16[256,1536]{1,0:T(8,128)(2,1)} %add_convert_fusion.4), channel_id=1, source_target_pairs={{0,2},{2,0},{1,3},{3,1},{4,6},{6,4},{5,7},{7,5},{8,10},{10,8},{9,1... | collective-permute-start | bytes 2359304 | tf_op jit(solution)/shard_map/ppermute | solution.py:604
  (165 other events, 1744.4 us)
